TPU v7x, 32 devices: a whole 2x2x4 slice. The times are simulated.
32 devices in a mesh: dp: 4 (over x, core), cent: 8 (over z, y).
Axes of the slice: x: 2, y: 2, z: 4, core: 2. Of those that a mesh axis runs over, the one named last changes fastest.
Arguments:
- embeddings: bfloat16 [4096, 4096], P('dp', 'cent'), may hold values from -6 to 6
- centroids: bfloat16 [4096, 4096], P('cent'), may hold values from -0.1875 to 0.1875
- assignment: int32 [4096], P('dp'), may hold values from 0 to 4095, as said below
- prior_counts: int32 [4096], P('cent'), may hold values from 1 to 4
Outputs:
- top_score: float32 [4096], P('dp')
- updated: float32 [4096, 4096], P('dp', 'cent')
Inputs may be any that keep to these rules, and one draw needn't show every extreme that they name: `assignment`: cluster k belongs to index k // 512 of cent. Among the 1024 rows of one index of dp, at most 256 have clusters that belong to one index of cent, and in every such block of rows some index of cent gets exactly 256 of them.
All inputs are finite; a program needn't handle non-finite values.
Results may differ from a plain program's by a relative error of at most 0.0003.
Values may be sent and summed in bfloat16 or wider, within the bound.
No kernel may reach another device: no remote copies, remote signals or barrier semaphores. Data moves between devices by JAX's collectives and lax.ppermute only.
A program may use at most 64 MiB of HBM per device.

v0:
```python
import jax
import jax.numpy as jnp
from jax import lax
from jax.sharding import PartitionSpec as P


def on_device(embeddings, centroids, assignment, prior_counts):
    whole = lax.all_gather(embeddings, "cent", axis=1, tiled=True)
    width = centroids.shape[0]
    half_norm = 0.5 * jnp.sum(jnp.square(centroids.astype(jnp.float32)), axis=1)
    score = (
        lax.dot_general(
            whole, centroids, (((1,), (1,)), ((), ())), preferred_element_type=jnp.float32
        )
        - half_norm[None, :]
    )
    top_score = lax.pmax(jnp.max(score, axis=1), "cent")
    owned = lax.axis_index("cent") * width + jnp.arange(width, dtype=jnp.int32)
    slice_width = whole.shape[1] // lax.axis_size("dp")
    match = assignment[:, None] == owned[None, :]
    onehot = match.astype(jnp.bfloat16)
    sums = lax.psum_scatter(
        lax.dot_general(
            whole, onehot, (((0,), (0,)), ((), ())), preferred_element_type=jnp.float32
        ),
        "dp",
        scatter_dimension=0,
        tiled=True,
    )
    counts = lax.psum(jnp.sum(match, axis=0, dtype=jnp.float32), "dp")
    own_slice = (
        lax.dynamic_slice_in_dim(centroids, lax.axis_index("dp") * slice_width, slice_width, 1)
        .astype(jnp.float32)
        .T
    )
    prior = prior_counts.astype(jnp.float32)
    updated = (prior[None, :] * own_slice + sums) / (prior + counts)[None, :]
    return (top_score, updated)


def solution(mesh):
    placed = (P("dp", "cent"), P("cent", None), P("dp"), P("cent"))
    return jax.shard_map(
        on_device, mesh=mesh, in_specs=placed, out_specs=(P("dp"), P("dp", "cent")), check_vma=False
    )
```

profile of v0, /device:TPU:0, one launch (start us, length us, event | category | flops | bytes accessed | tf_op | source)
XLA Modules:
  0.0 229.5 jit_solution(3113302570606261272)
XLA Ops:
  7.2 0.0 all-gather.2.cloned.1.call-start
  7.2 0.7 all-gather.2.cloned.1.call-update
  7.9 0.0 reduce-scatter.2.cloned.1.call-start
  8.0 130.2 %all-gather.2.cloned.1.call-done = bf16[1024,4096]{1,0:T(8,128)(2,1)} async-done(((bf16[1024,512]{1,0:T(8,128)(2,1)}), bf16[1024,4096]{1,0:T(8,128)(2,1)}) %all-gather.2.cloned.1.call-update) | async-done | bytes 8388624 | tf_op jit(solution)/shard_map/all_gather | solution.py:8
  138.2 10.4 %convolution_bitcast_fusion = f32[4096,512]{0,1:T(8,128)} fusion(bf16[1024,4096]{1,0:T(8,128)(2,1)} %all-gather.2.cloned.1.call-done, s32[512]{0:T(512)S(1)} %iota_add_fusion, s32[1024]{0:T(1024)} %param.6), kind=kOutput, calls=%fused_computation.1 | convolution fusion | flops 4295491584 | bytes 16783360 | tf_op jit(solution)/shard_map/dot_general | solution.py:23
  148.5 0.0 copy-start.1
  148.5 0.0 copy-start.2
  148.5 0.0 reduce-scatter.2.cloned.1.call-update
  148.6 0.6 copy-done.1
  149.2 0.0 copy-done.2
  149.2 0.3 fusion.2
  149.5 6.2 %psum.7 = f32[512]{0:T(512)S(1)} all-reduce(f32[512]{0:T(512)S(1)} %fusion.2), channel_id=1, replica_groups=mesh['dp'=4,'cent'=8] {'dp'}, use_global_device_ids=true, to_apply=%region_5.0 | all-reduce | flops 512 | bytes 4096 | tf_op jit(solution)/shard_map/psum | solution.py:30
  155.7 0.0 copy-start
  155.7 4.2 %multiply_reduce_fusion = f32[512]{0:T(512)S(1)} fusion(bf16[512,4096]{1,0:T(8,128)(2,1)} %param.5), kind=kLoop, calls=%fused_computation | loop fusion | flops 6290944 | bytes 4196352 | tf_op jit(solution)/shard_map/reduce_sum | solution.py:10
  159.9 1.2 copy-done
  161.1 8.2 %subtract_reduce_fusion = f32[1024]{0:T(1024)S(1)} fusion(bf16[1024,4096]{1,0:T(8,128)(2,1)} %all-gather.2.cloned.1.call-done, bf16[512,4096]{1,0:T(8,128)(2,1)S(1)} %copy-done, f32[512]{0:T(512)S(1)} %broadcast_multiply_fusion), kind=kOutput, calls=%fused_computation.8 | convolution fusion | flops 4296014848 | bytes 12589056 | tf_op jit(solution)/shard_map/dot_general | solution.py:12
  169.3 20.5 %pmax.7 = f32[1024]{0:T(1024)} all-reduce(f32[1024]{0:T(1024)S(1)} %subtract_reduce_fusion), channel_id=1, replica_groups=mesh['dp'=4,'cent'=8] {'cent'}, use_global_device_ids=true, to_apply=%region_2.0 | all-reduce | flops 1024 | bytes 8192 | tf_op jit(solution)/shard_map/pmax | solution.py:17
  189.8 28.8 %reduce-scatter.2.cloned.1.call-done = f32[1024,512]{0,1:T(8,128)} async-done(((f32[4096,512]{0,1:T(8,128)}), f32[1024,512]{0,1:T(8,128)}) %reduce-scatter.2.cloned.1.call-update) | async-done | bytes 2097168 | tf_op jit(solution)/shard_map/reduce_scatter | solution.py:22
  218.6 2.2 fusion.3
  220.8 1.8 copy.7
  (4 shorter events, 0.0 us)
Async XLA Ops:
  7.2 131.0 %all-gather.2.cloned.1.call-start = ((), (), s32[]{:S(2)}) async-start(), calls=%async_computation.1 | async-start | bytes 9437184 | tf_op jit(solution)/shard_map/all_gather | solution.py:8
  7.9 210.7 %reduce-scatter.2.cloned.1.call-start = ((), (), s32[]{:S(2)}) async-start(), calls=%async_computation.2 | async-start | bytes 10485760 | tf_op jit(solution)/shard_map/reduce_scatter | solution.py:22
  148.5 0.7 copy-start.1
  148.5 0.7 copy-start.2
  155.7 5.5 %copy-start = (bf16[512,4096]{1,0:T(8,128)(2,1)S(1)}, bf16[512,4096]{1,0:T(8,128)(2,1)}, u32[]{:S(2)}) copy-start(bf16[512,4096]{1,0:T(8,128)(2,1)} %param.5) | copy-start | bytes 12582916
Sparse Core Ops, SparseCore 0:
  10.0 128.0 all-gather.1
  148.7 69.8 reduce-scatter.1
where the time goes:
time: 230 us; the launch traced here: 229 us
  waiting for transfers between devices  160 us (70%)
  blocking collectives  26.6 us (12%)
  matrix products  18.6 us (8%)
  between operations  14.1 us (6%)
  other arithmetic  6.7 us (3%)
  local copies, waits for them, and re-layouts  3.72 us (2%)
    all_gather x1, waiting for transfers between devices, on_device(): whole = lax.all_gather(embeddings, 'cent', axis=1, tiled=True)  130 us
    reduce_scatter x1, waiting for transfers between devices, on_device(): lax.psum_scatter(lax.dot_general(whole, onehot, (((0,), (0,)), ((), ())),...  28.8 us
    pmax x1, blocking collectives, on_device(): top_score = lax.pmax(jnp.max(score, axis=1), 'cent')  20.5 us
    dot_general x1, matrix products, on_device(): lax.dot_general(whole, onehot, (((0,), (0,)), ((), ())), preferred_elemen...  10.4 us
    dot_general x1, matrix products, on_device(): lax.dot_general(whole, centroids, (((1,), (1,)), ((), ())), preferred_ele...  8.2 us
    psum x1, blocking collectives, on_device(): counts = lax.psum(jnp.sum(match, axis=0, dtype=jnp.float32), 'dp')  6.16 us
  transfers between devices with their start and end apart: 2, of which 2 were waited for; matrix products, arithmetic and copies ran while one was open for 6% of the time, Pallas kernels for 0%

commit v1 on v0

v1 whole, which is shorter than its diff:
```python
import jax
import jax.numpy as jnp
from jax import lax
from jax.experimental import pallas as pl
from jax.experimental.pallas import tpu as pltpu
from jax.sharding import PartitionSpec as P

VMEM = pl.BlockSpec(memory_space=pltpu.VMEM)
SMEM = pl.BlockSpec(memory_space=pltpu.SMEM)
PARAMS = pltpu.CompilerParams(vmem_limit_bytes=16 * 1024 * 1024)

ABOVE, HERE, BELOW = 0, 1, 2


class Steps:
    def __init__(self):
        self.token = jnp.zeros((8, 128), jnp.int32)

    def tie(self, *values):
        self.token, values = lax.optimization_barrier((self.token, values))
        return values[0] if len(values) == 1 else values


def chosen_rows(shift, first, count, half):
    at = lax.broadcasted_iota(jnp.int32, (count, half), 0) + (shift + first)
    at = jnp.where(at >= half, at - half, at)
    at = jnp.where(at >= half, at - half, at)
    hit = at == lax.broadcasted_iota(jnp.int32, (count, half), 1)
    return hit.astype(jnp.float32).astype(jnp.bfloat16)


def product(hot, rows):
    return jnp.dot(hot, rows, preferred_element_type=jnp.float32)


def between(starts_ref, has, wants, half):
    start = 0 if has is None else starts_ref[has]
    return lax.rem(starts_ref[wants] - start + 2 * half, half)


def turn(parts, starts, has, wants, first, count, split):
    half = sum(p.shape[0] for p in parts) if split else parts[0].shape[0]
    width = parts[0].shape[1] if split else sum(p.shape[1] for p in parts)

    def kernel(starts_ref, *refs):
        out_ref = refs[-1]
        hot = chosen_rows(between(starts_ref, has, wants, half), first, count, half)
        if split:
            near = refs[0].shape[0]
            total = product(hot[:, :near], refs[0][...]) + product(hot[:, near:], refs[1][...])
            out_ref[...] = total.astype(jnp.bfloat16)
        else:
            low = 0
            for ref in refs[:-1]:
                high = low + ref.shape[1]
                out_ref[:, low:high] = product(hot, ref[...]).astype(jnp.bfloat16)
                low = high

    return pl.pallas_call(
        kernel,
        in_specs=[SMEM] + [VMEM] * len(parts),
        out_specs=VMEM,
        out_shape=jax.ShapeDtypeStruct((count, width), jnp.bfloat16),
        compiler_params=PARAMS,
        cost_estimate=pl.CostEstimate(
            flops=2 * count * half * width, bytes_accessed=4 * half * width, transcendentals=0
        ),
        name="turn",
    )(starts, *parts)


def turn_down(kept, swapped, starts, near):
    half, width = kept.shape

    def kernel(starts_ref, kept_ref, swapped_ref, near_ref, far_ref):
        for n, (ref, has) in enumerate(((kept_ref, ABOVE), (swapped_ref, None))):
            hot = chosen_rows(between(starts_ref, has, BELOW, half), 0, half, half)
            rows = product(hot, ref[...]).astype(jnp.bfloat16)
            near_ref[:, n * width : (n + 1) * width] = rows[:near]
            far_ref[:, n * width : (n + 1) * width] = rows[near:]

    return pl.pallas_call(
        kernel,
        in_specs=[SMEM, VMEM, VMEM],
        out_specs=[VMEM, VMEM],
        out_shape=[
            jax.ShapeDtypeStruct((near, 2 * width), jnp.bfloat16),
            jax.ShapeDtypeStruct((half - near, 2 * width), jnp.bfloat16),
        ],
        compiler_params=PARAMS,
        cost_estimate=pl.CostEstimate(
            flops=4 * half * half * width, bytes_accessed=8 * half * width, transcendentals=0
        ),
        name="turn_down",
    )(starts, kept, swapped)


def take_share(ids, table, n_dp, late):
    count, depth = table.shape[0] // n_dp // (2 if late else 1), table.shape[1]

    def kernel(ids_ref, in_ref, out_ref):
        out_ref[...] = in_ref[...]

    return pl.pallas_call(
        kernel,
        grid_spec=pltpu.PrefetchScalarGridSpec(
            num_scalar_prefetch=1,
            grid=(1,),
            in_specs=[
                pl.BlockSpec(
                    (count, depth),
                    lambda g, ids: (2 * (ids[0] ^ (n_dp // 2)) + 1 if late else ids[0], 0),
                )
            ],
            out_specs=VMEM,
        ),
        out_shape=jax.ShapeDtypeStruct((count, depth), table.dtype),
        compiler_params=PARAMS,
        cost_estimate=pl.CostEstimate(
            flops=0, bytes_accessed=4 * count * depth, transcendentals=0
        ),
        name="take_share",
    )(ids, table)


def prepare(ids, starts, clusters, orders, kept, swapped, prior, table, cap):
    half, width = kept.shape
    n_dp, rows = clusters.shape
    own, feats = table.shape[0], table.shape[1] // n_dp

    def kernel(ids_ref, starts_ref, cluster_ref, order_ref, kept_ref, swapped_ref, prior_ref,
               table_ref, self_a, self_b, same_ref, across_ref, counts_ref, base_ref):
        for out_ref, ref, has in ((self_a, kept_ref, ABOVE), (self_b, swapped_ref, None)):
            hot = chosen_rows(between(starts_ref, has, HERE, half), 0, half, half)
            out_ref[...] = product(hot, ref[...]).astype(jnp.bfloat16)
        me = ids_ref[1]
        side, place = me & 1, me >> 1
        counts = jnp.zeros((1, own), jnp.float32)
        slot = lax.broadcasted_iota(jnp.int32, (cap, rows), 0)
        column = lax.broadcasted_iota(jnp.int32, (cap, own), 1).astype(jnp.float32)
        for m in range(n_dp):
            order, cluster = order_ref[m : m + 1, :], cluster_ref[m : m + 1, :]
            local = cluster - me * own
            local = jnp.where((local >= 0) & (local < own), local, own).astype(jnp.float32)
            earlier = (cluster < (2 * place + 1) * own).astype(jnp.float32)
            before = jnp.sum(earlier, axis=1, keepdims=True).astype(jnp.int32)
            for b, out_ref in enumerate((same_ref, across_ref)):
                which = side if b == 0 else 1 - side
                start = ((before + 1 - which) >> 1) - cap + half
                turned = (order >> 1) - start + 2 * half
                turned = jnp.where(turned >= 2 * half, turned - 2 * half, turned)
                turned = jnp.where(turned >= half, turned - half, turned)
                spot = jnp.where((order & 1) == which, turned - side * cap, rows)
                name = jnp.sum(jnp.where(slot == spot, local, 0.0), axis=1, keepdims=True)
                match = (column == name).astype(jnp.float32)
                out_ref[m * cap : (m + 1) * cap, :] = match.astype(jnp.bfloat16)
                counts = counts + jnp.sum(match, axis=0, keepdims=True)
        counts_ref[...] = counts
        base_ref[...] = table_ref[...].astype(jnp.float32).T * prior_ref[...]

    outs = [
        jax.ShapeDtypeStruct((half, width), jnp.bfloat16),
        jax.ShapeDtypeStruct((half, width), jnp.bfloat16),
        jax.ShapeDtypeStruct((n_dp * cap, own), jnp.bfloat16),
        jax.ShapeDtypeStruct((n_dp * cap, own), jnp.bfloat16),
        jax.ShapeDtypeStruct((1, own), jnp.float32),
        jax.ShapeDtypeStruct((feats, own), jnp.float32),
    ]
    return pl.pallas_call(
        kernel,
        grid_spec=pltpu.PrefetchScalarGridSpec(
            num_scalar_prefetch=2,
            grid=(1,),
            in_specs=[VMEM] * 5 + [pl.BlockSpec((own, feats), lambda g, ids, at: (0, ids[0]))],
            out_specs=[VMEM] * len(outs),
        ),
        out_shape=outs,
        compiler_params=PARAMS,
        cost_estimate=pl.CostEstimate(
            flops=4 * half * half * width, bytes_accessed=16 * half * width, transcendentals=0
        ),
        name="prepare",
    )(ids, starts, clusters, orders, kept, swapped, prior, table)


def collect(ids, windows, cap, n_dp):
    n_windows, per_dp = len(windows), len(windows) // n_dp
    wide = sum(part.shape[1] for part in windows[0])
    counts = [len(window) for window in windows]
    parts = [part for window in windows for part in window]

    def kernel(ids_ref, *refs):
        part_refs, out_refs = refs[: len(parts)], refs[len(parts) :]
        side, place = ids_ref[1] & 1, ids_ref[1] >> 1
        for m in range(n_dp):
            for e in range(per_dp):
                start = 0
                wanted = lax.rem(place - (ids_ref[0] ^ m) * per_dp - e + n_windows, n_windows)
                for n, count in enumerate(counts):

                    @pl.when(wanted == n)
                    def _(m=m, e=e, start=start, count=count):
                        low = e * wide
                        for ref in part_refs[start : start + count]:
                            high = low + ref.shape[1]
                            for b in (0, 1):
                                which = side if b == 0 else 1 - side
                                rows = pl.ds(pl.multiple_of(which * cap, cap), cap)
                                out_refs[2 * m + b][:, low:high] = ref[rows, :]
                            low = high

                    start += count

    outs = [jax.ShapeDtypeStruct((cap, per_dp * wide), jnp.bfloat16)] * (2 * n_dp)
    found = pl.pallas_call(
        kernel,
        in_specs=[SMEM] + [VMEM] * len(parts),
        out_specs=[VMEM] * len(outs),
        out_shape=outs,
        compiler_params=PARAMS,
        cost_estimate=pl.CostEstimate(
            flops=0, bytes_accessed=8 * n_dp * cap * per_dp * wide, transcendentals=0
        ),
        name="collect",
    )(ids, *parts)
    return {(m, b): found[2 * m + b] for m in range(n_dp) for b in (0, 1)}


def update(ids, same_rows, across_rows, same, across, base, prior, counts, token):
    n_rows, cap = len(same_rows), same_rows[0].shape[0]
    feats, own = base.shape
    width = feats // 2

    def kernel(ids_ref, *refs):
        same_refs, across_refs = refs[:n_rows], refs[n_rows : 2 * n_rows]
        same_ref, across_ref, base_ref, prior_ref, counts_ref, token_ref, out_ref = refs[
            2 * n_rows :
        ]
        nothing = token_ref[:1, :1].astype(jnp.float32)
        inverse = 1.0 / (prior_ref[...] + counts_ref[...] + nothing)
        step = pl.program_id(0)
        for n in (0, 1):

            @pl.when(step == n)
            def _(n=n):
                total = base_ref[...]
                for row_refs, match_ref, part in (
                    (same_refs, same_ref, n),
                    (across_refs, across_ref, 1 - n),
                ):
                    held = jnp.concatenate(
                        [ref[:, part * width : (part + 1) * width] for ref in row_refs], axis=0
                    )
                    total += lax.dot_general(
                        held,
                        match_ref[...],
                        (((0,), (0,)), ((), ())),
                        preferred_element_type=jnp.float32,
                    )
                out_ref[...] = total * inverse

    block = pl.BlockSpec((width, own), lambda g, ids: (g ^ (ids[1] & 1), 0))
    return pl.pallas_call(
        kernel,
        grid_spec=pltpu.PrefetchScalarGridSpec(
            num_scalar_prefetch=1,
            grid=(2,),
            in_specs=[VMEM] * (2 * n_rows + 2) + [block, VMEM, VMEM, VMEM],
            out_specs=block,
        ),
        out_shape=jax.ShapeDtypeStruct((feats, own), jnp.float32),
        compiler_params=PARAMS,
        cost_estimate=pl.CostEstimate(
            flops=4 * n_rows * cap * feats * own, bytes_accessed=8 * feats * own, transcendentals=0
        ),
        name="update",
    )(ids, *same_rows, *across_rows, same, across, base, prior, counts, token)


def column_block(n_line, steps):
    def block(g, ids):
        side, place = ids[1] & 1, ids[1] >> 1
        step = steps[-1]
        for n, other in enumerate(steps[:-1]):
            step = jnp.where(g // 2 == n, other, step)
        return 2 * lax.rem(place - step + n_line, n_line) + (side ^ (g % 2))

    return block


def score_part(ids, tables, work, half, n_line, so_far=None):
    sizes = [table.shape[0] for table in tables]
    total, width = sum(sizes), tables[0].shape[1] // (2 * n_line)
    n_tables, n_blocks = len(tables), 2 * len(work)
    block = column_block(n_line, [step for step, _ in work])
    parts = [part for _, piece in work for part in piece]
    before = [] if so_far is None else [so_far]

    def kernel(ids_ref, *refs):
        table_refs, part_refs = refs[:n_tables], list(refs[n_tables : n_tables + len(parts)])
        before_refs = refs[n_tables + len(parts) : -5]
        out_ref, best_ref, piece, score, squares = refs[-5:]
        step = pl.program_id(0)

        @pl.when(step == 0)
        def _():
            score[...] = before_refs[0][...] if before_refs else jnp.zeros_like(score)
            squares[...] = jnp.zeros_like(squares)

        for at, (_, held) in enumerate(work):
            held_refs = [part_refs.pop(0) for _ in held]
            for n in (0, 1):

                @pl.when(step == 2 * at + n)
                def _(n=n, held_refs=held_refs):
                    if held_refs[0].shape[1] == width:
                        piece[...] = held_refs[n][...]
                    else:
                        low = 0
                        for ref in held_refs:
                            high = low + ref.shape[0]
                            piece[low:high] = ref[:, n * width : (n + 1) * width]
                            low = high
                        if low < half:
                            piece[low:] = jnp.zeros((half - low, width), piece.dtype)

        low = 0
        for ref, size in zip(table_refs, sizes):
            score[low : low + size] += lax.dot_general(
                ref[...], piece[...], (((1,), (1,)), ((), ())), preferred_element_type=jnp.float32
            )
            for lane in range(0, width, 128):
                entries = ref[:, lane : lane + 128].astype(jnp.float32)
                squares[low : low + size] += entries * entries
            low += size

        @pl.when(step == n_blocks - 1)
        def _():
            final = score[...] - 0.5 * jnp.sum(squares[...], axis=1, keepdims=True)
            out_ref[...] = final
            best_ref[...] = jnp.max(final, axis=0, keepdims=True)

    grid_spec = pltpu.PrefetchScalarGridSpec(
        num_scalar_prefetch=1,
        grid=(n_blocks,),
        in_specs=[
            pl.BlockSpec((size, width), lambda g, ids: (0, block(g, ids))) for size in sizes
        ]
        + [VMEM] * (len(parts) + len(before)),
        out_specs=[VMEM, VMEM],
        scratch_shapes=[
            pltpu.VMEM((half, width), jnp.bfloat16),
            pltpu.VMEM((total, half), jnp.float32),
            pltpu.VMEM((total, 128), jnp.float32),
        ],
    )
    return pl.pallas_call(
        kernel,
        grid_spec=grid_spec,
        out_shape=[
            jax.ShapeDtypeStruct((total, half), jnp.float32),
            jax.ShapeDtypeStruct((1, half), jnp.float32),
        ],
        compiler_params=PARAMS,
        cost_estimate=pl.CostEstimate(
            flops=2 * half * total * width * n_blocks,
            bytes_accessed=2 * total * width * n_blocks,
            transcendentals=0,
        ),
        name="score_part",
    )(ids, *tables, *parts, *before)


def score_last(ids, starts, tables, last, scores, bests, order, near, n_line):
    count, width = last.shape[0], last.shape[1] // 2
    half, rows = scores[0].shape[1], order.shape[1]
    sizes = [table.shape[0] for table in tables]
    total, n_tables, n_scores = sum(sizes), len(tables), len(scores)
    block = column_block(n_line, [n_line // 2])
    low_row = near if near % 128 == 0 else 0

    def kernel(ids_ref, starts_ref, *refs):
        table_refs, last_ref = refs[:n_tables], refs[n_tables]
        score_refs = refs[n_tables + 1 : n_tables + 1 + n_scores]
        best_refs = refs[n_tables + 1 + n_scores : n_tables + 1 + 2 * n_scores]
        order_ref, out_ref, piece, sums = refs[n_tables + 1 + 2 * n_scores :]
        step = pl.program_id(0)
        if low_row < near:
            piece[: near - low_row] = jnp.zeros((near - low_row, width), piece.dtype)
        for n in (0, 1):

            @pl.when(step == n)
            def _(n=n):
                piece[near - low_row :] = last_ref[:, n * width : (n + 1) * width]

        low = 0
        for ref, size in zip(table_refs, sizes):
            part = lax.dot_general(
                ref[...], piece[...], (((1,), (1,)), ((), ())), preferred_element_type=jnp.float32
            )
            sums[low : low + size] = part + jnp.where(step == 0, 0.0, sums[low : low + size])
            low += size

        @pl.when(step == 1)
        def _():
            late, low = [], 0
            for ref in score_refs:
                high = low + ref.shape[0]
                score = sums[low:high] + ref[:, low_row:]
                late.append(jnp.max(score, axis=0, keepdims=True))
                low = high
            row = largest_of(late)
            if low_row:
                first = largest_of([ref[:, :low_row] for ref in best_refs])
                row = jnp.concatenate([first, row], axis=1)
            column = jnp.broadcast_to(row, (8, half)).T[:, :1]
            side = ids_ref[1] & 1
            order = order_ref[...]
            turned = (order >> 1) - starts_ref[HERE] + 2 * half
            turned = jnp.where(turned >= 2 * half, turned - 2 * half, turned)
            turned = jnp.where(turned >= half, turned - half, turned)
            ours = (order & 1) == side
            found = lax.broadcasted_iota(jnp.int32, (half, rows), 0) == turned
            best = jnp.sum(jnp.where(found, column, 0.0), axis=0, keepdims=True)
            out_ref[...] = jnp.where(ours, best, -jnp.inf)

    grid_spec = pltpu.PrefetchScalarGridSpec(
        num_scalar_prefetch=2,
        grid=(2,),
        in_specs=[
            pl.BlockSpec((size, width), lambda g, ids, at: (0, block(g, ids))) for size in sizes
        ]
        + [VMEM] * (2 + 2 * n_scores),
        out_specs=VMEM,
        scratch_shapes=[
            pltpu.VMEM((half - low_row, width), jnp.bfloat16),
            pltpu.VMEM((total, half - low_row), jnp.float32),
        ],
    )
    return pl.pallas_call(
        kernel,
        grid_spec=grid_spec,
        out_shape=jax.ShapeDtypeStruct((1, rows), jnp.float32),
        compiler_params=PARAMS,
        cost_estimate=pl.CostEstimate(
            flops=4 * count * total * width, bytes_accessed=4 * total * width, transcendentals=0
        ),
        name="score_last",
    )(ids, starts, *tables, last, *scores, *bests, order)


def on_device(embeddings, centroids, assignment, prior_counts):
    n_dp, n_cent = lax.axis_size("dp"), lax.axis_size("cent")
    rows, width = embeddings.shape
    own, depth = centroids.shape
    half, n_line = rows // 2, n_cent // 2
    per_dp = n_line // n_dp
    cap = rows // n_cent
    near = 2 * cap
    middle = n_line // 2
    me_dp, me = lax.axis_index("dp"), lax.axis_index("cent")
    side, place = me % 2, me // 2
    swap = [(j, j ^ 1) for j in range(n_cent)]

    def ring(shift):
        return [(j, (j + 2 * shift) % n_cent) for j in range(n_cent)]

    def send(value, pairs):
        return lax.ppermute(value, "cent", pairs)

    ids = jnp.stack([me_dp, me])
    owner_of = assignment // own
    key = owner_of * rows + jnp.arange(rows, dtype=jnp.int32)
    order = jnp.sum(key[None, :] < key[:, None], axis=1, dtype=jnp.int32)
    parity, turn_no = order % 2, order // 2
    layers = (place + jnp.array([1, 0, n_line - 1], jnp.int32)) % n_line
    before = jnp.sum(owner_of[None, :] <= 2 * layers[:, None], axis=1, dtype=jnp.int32)
    starts = (before + 1 - side) // 2 - cap + half
    with jax.named_scope("deal_rows"):
        slot = jnp.where(parity == side, (turn_no - starts[ABOVE] + 2 * half) % half, half + turn_no)
        deal = jnp.arange(rows, dtype=jnp.int32)[:, None] == slot[None, :]
        dealt = lax.dot_general(
            deal.astype(jnp.bfloat16),
            embeddings,
            (((1,), (0,)), ((), ())),
            preferred_element_type=jnp.float32,
        ).astype(jnp.bfloat16)

    steps = Steps()
    kept, given, assignment, order, centroids, ids, starts = steps.tie(
        dealt[:half], dealt[half:], assignment, order, centroids, ids, starts
    )
    up_a, swapped = send(kept, ring(1)), send(given, swap)
    blocks = jnp.stack([assignment, order])[None]
    prior = prior_counts.astype(jnp.float32)[None, :]
    order = order[None, :]
    share = take_share(ids, centroids, n_dp, False)

    swapped, share, blocks, prior, order = steps.tie(swapped, share, blocks, prior, order)
    up_b, up_a = steps.tie(turn([swapped], starts, None, ABOVE, 0, half, False), up_a)
    up_b = send(up_b, ring(1))
    close, far, share = steps.tie(*turn_down(kept, swapped, starts, near), share)
    close, share = send(close, ring(-1)), send(share, swap)

    blocks, held_from = steps.tie(blocks), [0]
    bit = n_dp // 2
    while bit:
        pairs = [(d, d ^ bit) for d in range(n_dp)]
        blocks = jnp.concatenate([blocks, lax.ppermute(blocks, "dp", pairs)], axis=0)
        held_from = held_from + [m ^ bit for m in held_from]
        bit //= 2
        blocks = steps.tie(blocks)

    ids, centroids = steps.tie(ids, centroids)
    late_share = take_share(ids, centroids, n_dp, True)

    up_b, close, share, late_share = steps.tie(up_b, close, share, late_share)
    up = (up_a, up_b)
    pieces = {1: up}
    for step in range(2, middle):
        wide = send(turn(list(up), starts, HERE, ABOVE, 0, half, False), ring(1))
        up = (wide[:, :width], wide[:, width:])
        pieces[step] = up
    middle_near, share, late_share = steps.tie(
        turn(list(up), starts, HERE, ABOVE, 0, near, False), share, late_share
    )
    middle_near = send(middle_near, ring(1))

    others, bit = [share], n_dp // 2
    if n_dp == 4:
        pairs = [(d, d ^ bit) for d in range(n_dp)]
        others = [
            share,
            lax.ppermute(share[: share.shape[0] // 2], "dp", pairs),
            send(late_share, swap),
        ]
    else:
        while bit > 1:
            pairs = [(d, d ^ bit) for d in range(n_dp)]
            others = others + [lax.ppermute(p, "dp", pairs) for p in others]
            bit //= 2
    clusters, orders, centroids = steps.tie(blocks[:, 0], blocks[:, 1], centroids)
    self_a, self_b, same, across, counts, base = prepare(
        ids, starts, clusters, orders, kept, swapped, prior, centroids, cap
    )
    pieces[0] = (self_a, self_b)

    middle_near, pieces[0], same, across, counts, base = steps.tie(
        middle_near, pieces[0], same, across, counts, base
    )
    far = send(steps.tie(far), ring(-1))
    windows = dict(pieces)
    windows[middle], windows[n_line - 1] = (middle_near,), (close,)

    down = (close, far)
    downs = {n_line - 1: down}

    def deliver(value, m, b):
        pairs = [
            (d * n_cent + j, (d ^ m) * n_cent + (j ^ b)) for d in range(n_dp) for j in range(n_cent)
        ]
        return lax.ppermute(value, ("dp", "cent"), pairs)

    for step in range(2, middle):
        down = tuple(
            send(turn(list(down), starts, HERE, BELOW, first, count, True), ring(-1))
            for first, count in ((0, near), (near, half - near))
        )
        downs[n_line - step] = down
        windows[n_line - step] = (down[0],)
    first = [(m, 0) for m in range(2, n_dp)] + [(0, 1), (1, 1)]
    second = [(m, 1) for m in range(2, n_dp)] + [(1, 0)]
    got = steps.tie(collect(ids, [windows[n] for n in range(n_line)], cap, n_dp))
    others = steps.tie(others)
    core_sent = steps.tie(jnp.concatenate(others, axis=0))
    core = lax.ppermute(core_sent, "dp", [(d, d ^ 1) for d in range(n_dp)])
    for key in first:
        got[key] = deliver(got[key], *key)

    core, pieces = steps.tie(core, pieces)
    tables = [centroids, core_sent, core]
    work = [(step, pieces[step]) for step in pieces] + [(middle, (middle_near,))]
    so_far, _ = score_part(ids, tables, work, half, n_line)
    so_far = steps.tie(so_far)
    got.update(zip(first, steps.tie(*[got[key] for key in first])))

    downs[n_line - 1] = (close, steps.tie(downs[n_line - 1][1]))
    middle_far = steps.tie(
        turn(list(downs[middle + 1]), starts, HERE, BELOW, near, half - near, True)
    )
    middle_far = send(middle_far, ring(-1))
    for key, value in zip(second, steps.tie(*[got[key] for key in second])):
        got[key] = deliver(value, *key)
    downs = steps.tie(downs)
    work = [(step, downs[step]) for step in downs]
    score, best = steps.tie(*score_part(ids, tables, work, half, n_line, so_far))

    middle_far, got[1, 0] = steps.tie(middle_far, got[1, 0])
    best = score_last(
        ids, starts, tables, middle_far, [score], [best], order, near, n_line
    )[0]
    best = steps.tie(best)
    arrived = [send(best, ring(step)) for step in range(1, n_line)]

    got = steps.tie(got)
    feats = 2 * per_dp * width
    if per_dp == 1:
        updated = update(
            ids,
            [got[m, 0] for m in held_from],
            [got[m, 1] for m in held_from],
            same,
            across,
            base,
            prior,
            counts,
            steps.token,
        )
    else:
        counts = counts + steps.token[0, 0].astype(jnp.float32)

        def summed(match, b):
            held = jnp.concatenate([got[m, b] for m in held_from], axis=0)
            total = lax.dot_general(
                held, match, (((0,), (0,)), ((), ())), preferred_element_type=jnp.float32
            )
            return total.reshape(per_dp, 2, width, own)

        from_same, from_across = summed(same, 0), summed(across, 1)
        mine = from_same[:, 0] + from_across[:, 1]
        theirs = from_same[:, 1] + from_across[:, 0]
        even = jnp.where(side == 0, mine, theirs)
        odd = jnp.where(side == 0, theirs, mine)
        sums = jnp.stack([even, odd], axis=1).reshape(base.shape)
        updated = (base + sums) / (prior + counts)
    best, updated = steps.tie(best, updated)
    best = largest_of([best] + arrived)
    return (jnp.maximum(best, send(best, swap)), updated)


def largest_of(values):
    largest = values[0]
    for value in values[1:]:
        largest = jnp.maximum(largest, value)
    return largest


def solution(mesh):
    placed = (P("dp", "cent"), P("cent", None), P("dp"), P("cent"))
    return jax.shard_map(
        on_device, mesh=mesh, in_specs=placed, out_specs=(P("dp"), P("dp", "cent")), check_vma=False
    )
```

time: 230 us -> 113 us (0.49)
  waiting for transfers between devices: 160 us -> 55.8 us
  blocking collectives: 26.6 us -> 0 us
  starting transfers between devices: 0.08 us -> 26.1 us
  Pallas kernels: 0 us -> 25.5 us
  matrix products: 18.6 us -> 1.26 us
  between operations: 14.1 us -> 0.89 us
  other arithmetic: 6.7 us -> 3.11 us
  local copies, waits for them, and re-layouts: 3.72 us -> 0.17 us
    all_gather x1 -> x0, waiting for transfers between devices: 130 us -> none  [on_device(): whole = lax.all_gather(embeddings, 'cent', axis=1, tiled=True)]
    ppermute x0 -> x24, waiting for transfers between devices: none -> 55.8 us  [the longest x13 48.4 us: send(): return lax.ppermute(value, 'cent', pairs)]
    reduce_scatter x1 -> x0, waiting for transfers between devices: 28.8 us -> none  [on_device(): lax.psum_scatter(lax.dot_general(whole, onehot, (((0,), (0,)), ((), ())),...]
    ppermute x0 -> x24, starting transfers between devices: none -> 26.1 us  [the longest x13 17 us: send(): return lax.ppermute(value, 'cent', pairs)]
    pallas_call x0 -> x12, Pallas kernels: none -> 25.5 us  [the longest x2 11.5 us: score_part(): pl.pallas_call(kernel, grid_spec=grid_spec, out_shape=[jax.ShapeDtypeStru...]
    pmax x1 -> x0, blocking collectives: 20.5 us -> none  [on_device(): top_score = lax.pmax(jnp.max(score, axis=1), 'cent')]
    dot_general x2 -> x1, matrix products: 18.6 us -> 1.26 us  [on_device(): lax.dot_general(deal.astype(jnp.bfloat16), embeddings, (((1,), (0,)), (()...]
    psum x1 -> x0, blocking collectives: 6.16 us -> none  [on_device(): counts = lax.psum(jnp.sum(match, axis=0, dtype=jnp.float32), 'dp')]
  transfers between devices with their start and end apart: 2 -> 24, of which waited for: 2 -> 15; matrix products, arithmetic and copies ran while one was open for 6% -> 0% of each run, Pallas kernels for 0% -> 21%
where the time goes in v1:
time: 113 us
  waiting for transfers between devices  55.8 us (49%)
  starting transfers between devices  26.1 us (23%)
  Pallas kernels  25.5 us (23%)
  other arithmetic  3.11 us (3%)
  matrix products  1.26 us (1%)
    ppermute x13, waiting for transfers between devices, send(): return lax.ppermute(value, 'cent', pairs)  48.4 us
    ppermute x13, starting transfers between devices, send(): return lax.ppermute(value, 'cent', pairs)  17 us
    pallas_call x2, Pallas kernels, score_part(): pl.pallas_call(kernel, grid_spec=grid_spec, out_shape=[jax.ShapeDtypeStru...  11.5 us
    ppermute x7, starting transfers between devices, deliver(): return lax.ppermute(value, ('dp', 'cent'), pairs)  5.99 us
    ppermute x7, waiting for transfers between devices, deliver(): return lax.ppermute(value, ('dp', 'cent'), pairs)  3.8 us
    ppermute x2, waiting for transfers between devices, on_device(): lax.ppermute(blocks, 'dp', pairs)  3.34 us
    pallas_call x1, Pallas kernels, update(): pl.pallas_call(kernel, grid_spec=pltpu.PrefetchScalarGridSpec(num_scalar_...  3.21 us
    pallas_call x3, Pallas kernels, turn(): pl.pallas_call(kernel, in_specs=[SMEM] + [VMEM] * len(parts), out_specs=V...  2.95 us
  transfers between devices with their start and end apart: 24, of which 15 were waited for; matrix products, arithmetic and copies ran while one was open for 0% of the time, Pallas kernels for 21%

profile of v1, /device:TPU:0, one launch (start us, length us, event | category | flops | bytes accessed | tf_op | source)
XLA Modules:
  0.0 112.8 jit_solution(6058073731737026706)
XLA Ops:
  4.4 3.0 %collective-permute-start = (bf16[512,512]{1,0:T(8,128)(2,1)S(1)}, bf16[512,512]{1,0:T(8,128)(2,1)S(1)}, u32[]{:S(2)}, u32[]{:S(2)}) collective-permute-start(bf16[512,512]{1,0:T(8,128)(2,1)S(1)} %get-tuple-element.133), channel_id=1, source_target_pairs={{0,1},{1,0},{2,3},{3,2},{4,5},{5,4},{6,7},{7,6},{8,9},{9,8},{10,11... | collective-permute-start | bytes 1572872 | tf_op jit(solution)/shard_map/ppermute | solution.py:469
  7.4 1.6 %collective-permute-start.1 = (bf16[512,512]{1,0:T(8,128)(2,1)S(1)}, bf16[512,512]{1,0:T(8,128)(2,1)S(1)}, u32[]{:S(2)}, u32[]{:S(2)}) collective-permute-start(bf16[512,512]{1,0:T(8,128)(2,1)S(1)} %get-tuple-element.141.kept_ref), channel_id=1, source_target_pairs={{0,2},{1,3},{2,4},{3,5},{4,6},{5,7},{6,0},{7,1},{8,10},{9,11},{10,... | collective-permute-start | bytes 1572872 | tf_op jit(solution)/shard_map/ppermute | solution.py:469
  9.6 9.7 %collective-permute-done.refs_0_.swapped_ref = bf16[512,512]{1,0:T(8,128)(2,1)S(1)} collective-permute-done((bf16[512,512]{1,0:T(8,128)(2,1)S(1)}, bf16[512,512]{1,0:T(8,128)(2,1)S(1)}, u32[]{:S(2)}, u32[]{:S(2)}) %collective-permute-start) | collective-permute-done | bytes 524320 | tf_op jit(solution)/shard_map/ppermute | solution.py:469
  23.4 1.6 %collective-permute-start.4 = (bf16[512,512]{1,0:T(8,128)(2,1)S(1)}, bf16[512,512]{1,0:T(8,128)(2,1)S(1)}, u32[]{:S(2)}, u32[]{:S(2)}) collective-permute-start(bf16[512,512]{1,0:T(8,128)(2,1)S(1)} %turn.3), channel_id=1, source_target_pairs={{0,2},{1,3},{2,4},{3,5},{4,6},{5,7},{6,0},{7,1},{8,10},{9,11},{10,... | collective-permute-start | bytes 1572872 | tf_op jit(solution)/shard_map/ppermute | solution.py:469
  25.0 2.3 %collective-permute-start.5 = (bf16[256,1024]{1,0:T(8,128)(2,1)S(1)}, bf16[256,1024]{1,0:T(8,128)(2,1)S(1)}, u32[]{:S(2)}, u32[]{:S(2)}) collective-permute-start(bf16[256,1024]{1,0:T(8,128)(2,1)S(1)} %get-tuple-element.155), channel_id=1, source_target_pairs={{0,6},{1,7},{2,0},{3,1},{4,2},{5,3},{6,4},{7,5},{8,14},{9,15},{10,... | collective-permute-start | bytes 1572872 | tf_op jit(solution)/shard_map/ppermute | solution.py:469
  27.2 1.5 %collective-permute-start.2 = (s32[1,2,1024]{2,1,0:T(2,128)S(1)}, s32[1,2,1024]{2,1,0:T(2,128)S(1)}, u32[]{:S(2)}, u32[]{:S(2)}) collective-permute-start(s32[1,2,1024]{2,1,0:T(2,128)S(1)} %add_bitcast_fusion), channel_id=1, source_target_pairs={{0,16},{8,24},{16,0},{24,8},{1,17},{9,25},{17,1},{25,9},{2,18},{10... | collective-permute-start | bytes 24584 | tf_op jit(solution)/shard_map/ppermute | solution.py:509
  28.7 2.2 %collective-permute-done.2 = s32[1,2,1024]{2,1,0:T(2,128)S(1)} collective-permute-done((s32[1,2,1024]{2,1,0:T(2,128)S(1)}, s32[1,2,1024]{2,1,0:T(2,128)S(1)}, u32[]{:S(2)}, u32[]{:S(2)}) %collective-permute-start.2) | collective-permute-done | bytes 8224 | tf_op jit(solution)/shard_map/ppermute | solution.py:509
  32.6 7.4 %collective-permute-done.4.refs_1_.refs_3_.refs_6_ = bf16[512,512]{1,0:T(8,128)(2,1)S(1)} collective-permute-done((bf16[512,512]{1,0:T(8,128)(2,1)S(1)}, bf16[512,512]{1,0:T(8,128)(2,1)S(1)}, u32[]{:S(2)}, u32[]{:S(2)}) %collective-permute-start.4) | collective-permute-done | bytes 524320 | tf_op jit(solution)/shard_map/ppermute | solution.py:469
  40.1 8.4 %collective-permute-done.5.refs_5_.refs_0_.refs_3_ = bf16[256,1024]{1,0:T(8,128)(2,1)S(1)} collective-permute-done((bf16[256,1024]{1,0:T(8,128)(2,1)S(1)}, bf16[256,1024]{1,0:T(8,128)(2,1)S(1)}, u32[]{:S(2)}, u32[]{:S(2)}) %collective-permute-start.5) | collective-permute-done | bytes 524320 | tf_op jit(solution)/shard_map/ppermute | solution.py:469
  50.6 1.6 %collective-permute-start.8 = (bf16[64,4096]{1,0:T(8,128)(2,1)S(1)}, bf16[64,4096]{1,0:T(8,128)(2,1)S(1)}, u32[]{:S(2)}, u32[]{:S(2)}) collective-permute-start(bf16[64,4096]{1,0:T(8,128)(2,1)S(1)} %slice.23), channel_id=1, source_target_pairs={{0,16},{8,24},{16,0},{24,8},{1,17},{9,25},{17,1},{25,9},{2,18},{10... | collective-permute-start | bytes 1572872 | tf_op jit(solution)/shard_map/ppermute | solution.py:534
  53.2 2.1 %prepare.1 = (bf16[512,512]{1,0:T(8,128)(2,1)S(1)}, bf16[512,512]{1,0:T(8,128)(2,1)S(1)}, bf16[512,512]{1,0:T(8,128)(2,1)S(1)}, bf16[512,512]{1,0:T(8,128)(2,1)S...) custom-call(s32[2]{0:T(128)S(1)} %pad_add_fusion.2.ids_ref, s32[3]{0:T(128)S(1)} %fusion.12.starts_ref, ...), custom_call_target="tpu_custom_call" | custom-call | flops 536870912 | bytes 4194304 | tf_op jit(solution)/shard_map/prepare/pallas_call | solution.py:169
  55.3 9.2 %collective-permute-done.7.refs_4_.refs_7_ = bf16[256,1024]{1,0:T(8,128)(2,1)S(1)} collective-permute-done((bf16[256,1024]{1,0:T(8,128)(2,1)S(1)}, bf16[256,1024]{1,0:T(8,128)(2,1)S(1)}, u32[]{:S(2)}, u32[]{:S(2)}) %collective-permute-start.7) | collective-permute-done | bytes 524320 | tf_op jit(solution)/shard_map/ppermute | solution.py:469
  65.7 2.1 %collective-permute-start.15 = (bf16[256,1024]{1,0:T(8,128)(2,1)S(1)}, bf16[256,1024]{1,0:T(8,128)(2,1)S(1)}, u32[]{:S(2)}, u32[]{:S(2)}) collective-permute-start(bf16[256,1024]{1,0:T(8,128)(2,1)S(1)} %get-tuple-element.215), channel_id=1, source_target_pairs={{0,6},{1,7},{2,0},{3,1},{4,2},{5,3},{6,4},{7,5},{8,14},{9,15},{10,... | collective-permute-start | bytes 1572872 | tf_op jit(solution)/shard_map/ppermute | solution.py:469
  69.9 1.4 %collective-permute-start.14 = (bf16[128,1024]{1,0:T(8,128)(2,1)S(1)}, bf16[128,1024]{1,0:T(8,128)(2,1)S(1)}, u32[]{:S(2)}, u32[]{:S(2)}) collective-permute-start(bf16[128,1024]{1,0:T(8,128)(2,1)S(1)} %get-tuple-element.213), channel_id=1, source_target_pairs={{0,9},{1,8},{2,11},{3,10},{4,13},{5,12},{6,15},{7,14},{8,1},{9,0},... | collective-permute-start | bytes 786440 | tf_op jit(solution)/shard_map/ppermute | solution.py:562
  71.3 8.3 %score_part.2 = (f32[1024,512]{1,0:T(8,128)S(1)}, f32[1,512]{1,0:T(1,128)}) custom-call(s32[2]{0:T(128)S(1)} %pad_add_fusion.2.ids_ref, bf16[512,4096]{1,0:T(8,128)(2,1)S(1)} %copy-done.1, bf16[256,4096]{1,0:T(8,128)(2,1)S(1)} %pad_maximum_fusion.refs_1_, bf16[256,4096]{1,0:T(8,128)(2,1)S(1)} %collective-permute-done.10.refs_2_, ...), custom_call_target="tpu_custom_call" | custom-call | flops 3221225472 | bytes 6291456 | tf_op jit(solution)/shard_map/score_part/pallas_call | solution.py:357
  79.6 1.4 %collective-permute-done.12.refs_3_ = bf16[128,1024]{1,0:T(8,128)(2,1)S(1)} collective-permute-done((bf16[128,1024]{1,0:T(8,128)(2,1)S(1)}, bf16[128,1024]{1,0:T(8,128)(2,1)S(1)}, u32[]{:S(2)}, u32[]{:S(2)}) %collective-permute-start.12) | collective-permute-done | bytes 262176 | tf_op jit(solution)/shard_map/ppermute | solution.py:562
  81.0 2.4 %collective-permute-done.14.refs_6_ = bf16[128,1024]{1,0:T(8,128)(2,1)S(1)} collective-permute-done((bf16[128,1024]{1,0:T(8,128)(2,1)S(1)}, bf16[128,1024]{1,0:T(8,128)(2,1)S(1)}, u32[]{:S(2)}, u32[]{:S(2)}) %collective-permute-start.14) | collective-permute-done | bytes 262176 | tf_op jit(solution)/shard_map/ppermute | solution.py:562
  85.3 2.4 %collective-permute-start.19 = (bf16[128,1024]{1,0:T(8,128)(2,1)S(1)}, bf16[128,1024]{1,0:T(8,128)(2,1)S(1)}, u32[]{:S(2)}, u32[]{:S(2)}) collective-permute-start(bf16[128,1024]{1,0:T(8,128)(2,1)S(1)} %get-tuple-element.245), channel_id=1, source_target_pairs={{0,25},{1,24},{2,27},{3,26},{4,29},{5,28},{6,31},{7,30},{8,17},{9,... | collective-permute-start | bytes 786440 | tf_op jit(solution)/shard_map/ppermute | solution.py:562
  87.7 3.2 %score_part.3 = (f32[1024,512]{1,0:T(8,128)S(1)}, f32[1,512]{1,0:T(1,128)S(1)}) custom-call(s32[2]{0:T(128)S(1)} %pad_add_fusion.2.ids_ref, bf16[512,4096]{1,0:T(8,128)(2,1)S(1)} %copy-done.1, bf16[256,4096]{1,0:T(8,128)(2,1)S(1)} %pad_maximum_fusion.refs_1_, bf16[256,4096]{1,0:T(8,128)(2,1)S(1)} %collective-permute-done.10.refs_2_, ...), custom_call_target="tpu_custom_call" | custom-call | flops 1073741824 | bytes 2097152 | tf_op jit(solution)/shard_map/score_part/pallas_call | solution.py:357
  90.8 7.6 %collective-permute-done.16.refs_3_ = bf16[256,1024]{1,0:T(8,128)(2,1)S(1)} collective-permute-done((bf16[256,1024]{1,0:T(8,128)(2,1)S(1)}, bf16[256,1024]{1,0:T(8,128)(2,1)S(1)}, u32[]{:S(2)}, u32[]{:S(2)}) %collective-permute-start.16) | collective-permute-done | bytes 524320 | tf_op jit(solution)/shard_map/ppermute | solution.py:469
  98.4 2.5 %score_last.1 = f32[1,1024]{1,0:T(1,128)S(1)} custom-call(s32[2]{0:T(128)S(1)} %pad_add_fusion.2.ids_ref, s32[3]{0:T(128)S(1)} %fusion.12.starts_ref, bf16[512,4096]{1,0:T(8,128)(2,1)S(1)} %copy-done.1, bf16[256,4096]{1,0:T(8,128)(2,1)S(1)} %pad_maximum_fusion.refs_1_, bf16[256,4096]{1,0:T(8,128)(2,1)S(1)} %collective-permute-done.10.refs_2_, ...), custom_call_target="tpu_custom_call" | custom-call | flops 536870912 | bytes 2097152 | tf_op jit(solution)/shard_map/score_last/pallas_call | solution.py:440
  101.0 2.2 %collective-permute-start.22 = (f32[1024]{0:T(1024)S(1)}, f32[1024]{0:T(1024)S(1)}, u32[]{:S(2)}, u32[]{:S(2)}) collective-permute-start(f32[1024]{0:T(1024)S(1)} %bitcast.20), channel_id=1, source_target_pairs={{0,6},{1,7},{2,0},{3,1},{4,2},{5,3},{6,4},{7,5},{8,14},{9,15},{10,... | collective-permute-start | bytes 12296 | tf_op jit(solution)/shard_map/ppermute | solution.py:469
  103.9 3.2 %update.1 = f32[1024,512]{1,0:T(8,128)} custom-call(s32[2]{0:T(128)S(1)} %pad_add_fusion.2.ids_ref, bf16[128,1024]{1,0:T(8,128)(2,1)S(1)} %get-tuple-element.248.refs_0_, bf16[128,1024]{1,0:T(8,128)(2,1)S(1)} %collective-permute-done.11.refs_1_, bf16[128,1024]{1,0:T(8,128)(2,1)S(1)} %collective-permute-done.17.refs_2_, ...), custom_call_target="tpu_custom_call" | custom-call | flops 1073741824 | bytes 4194304 | tf_op jit(solution)/shard_map/update/pallas_call | solution.py:263
  108.9 3.3 %collective-permute-done.23 = f32[1024]{0:T(1024)S(1)} collective-permute-done((f32[1024]{0:T(1024)S(1)}, f32[1024]{0:T(1024)S(1)}, u32[]{:S(2)}, u32[]{:S(2)}) %collective-permute-start.23) | collective-permute-done | bytes 4128 | tf_op jit(solution)/shard_map/ppermute | solution.py:469
  (64 shorter events, 21.5 us)
Async XLA Ops:
  4.4 14.9 %collective-permute-start = (bf16[512,512]{1,0:T(8,128)(2,1)S(1)}, bf16[512,512]{1,0:T(8,128)(2,1)S(1)}, u32[]{:S(2)}, u32[]{:S(2)}) collective-permute-start(bf16[512,512]{1,0:T(8,128)(2,1)S(1)} %get-tuple-element.133), channel_id=1, source_target_pairs={{0,1},{1,0},{2,3},{3,2},{4,5},{5,4},{6,7},{7,6},{8,9},{9,8},{10,11... | collective-permute-start | bytes 1572872 | tf_op jit(solution)/shard_map/ppermute | solution.py:469
  7.4 15.2 %collective-permute-start.1 = (bf16[512,512]{1,0:T(8,128)(2,1)S(1)}, bf16[512,512]{1,0:T(8,128)(2,1)S(1)}, u32[]{:S(2)}, u32[]{:S(2)}) collective-permute-start(bf16[512,512]{1,0:T(8,128)(2,1)S(1)} %get-tuple-element.141.kept_ref), channel_id=1, source_target_pairs={{0,2},{1,3},{2,4},{3,5},{4,6},{5,7},{6,0},{7,1},{8,10},{9,11},{10,... | collective-permute-start | bytes 1572872 | tf_op jit(solution)/shard_map/ppermute | solution.py:469
  22.6 25.8 %collective-permute-start.6 = (bf16[128,4096]{1,0:T(8,128)(2,1)S(1)}, bf16[128,4096]{1,0:T(8,128)(2,1)S(1)}, u32[]{:S(2)}, u32[]{:S(2)}) collective-permute-start(bf16[128,4096]{1,0:T(8,128)(2,1)S(1)} %take_share.2), channel_id=1, source_target_pairs={{0,1},{1,0},{2,3},{3,2},{4,5},{5,4},{6,7},{7,6},{8,9},{9,8},{10,11... | collective-permute-start | bytes 3145736 | tf_op jit(solution)/shard_map/ppermute | solution.py:469
  23.4 16.7 %collective-permute-start.4 = (bf16[512,512]{1,0:T(8,128)(2,1)S(1)}, bf16[512,512]{1,0:T(8,128)(2,1)S(1)}, u32[]{:S(2)}, u32[]{:S(2)}) collective-permute-start(bf16[512,512]{1,0:T(8,128)(2,1)S(1)} %turn.3), channel_id=1, source_target_pairs={{0,2},{1,3},{2,4},{3,5},{4,6},{5,7},{6,0},{7,1},{8,10},{9,11},{10,... | collective-permute-start | bytes 1572872 | tf_op jit(solution)/shard_map/ppermute | solution.py:469
  25.0 23.5 %collective-permute-start.5 = (bf16[256,1024]{1,0:T(8,128)(2,1)S(1)}, bf16[256,1024]{1,0:T(8,128)(2,1)S(1)}, u32[]{:S(2)}, u32[]{:S(2)}) collective-permute-start(bf16[256,1024]{1,0:T(8,128)(2,1)S(1)} %get-tuple-element.155), channel_id=1, source_target_pairs={{0,6},{1,7},{2,0},{3,1},{4,2},{5,3},{6,4},{7,5},{8,14},{9,15},{10,... | collective-permute-start | bytes 1572872 | tf_op jit(solution)/shard_map/ppermute | solution.py:469
  27.2 3.7 %collective-permute-start.2 = (s32[1,2,1024]{2,1,0:T(2,128)S(1)}, s32[1,2,1024]{2,1,0:T(2,128)S(1)}, u32[]{:S(2)}, u32[]{:S(2)}) collective-permute-start(s32[1,2,1024]{2,1,0:T(2,128)S(1)} %add_bitcast_fusion), channel_id=1, source_target_pairs={{0,16},{8,24},{16,0},{24,8},{1,17},{9,25},{17,1},{25,9},{2,18},{10... | collective-permute-start | bytes 24584 | tf_op jit(solution)/shard_map/ppermute | solution.py:509
  30.9 1.2 %collective-permute-start.3 = (s32[2,2,1024]{2,1,0:T(2,128)S(1)}, s32[2,2,1024]{2,1,0:T(2,128)S(1)}, u32[]{:S(2)}, u32[]{:S(2)}) collective-permute-start(s32[2,2,1024]{2,1,0:T(2,128)S(1)} %pad_add_fusion.1), channel_id=1, source_target_pairs={{0,8},{8,0},{16,24},{24,16},{1,9},{9,1},{17,25},{25,17},{2,10},{10... | collective-permute-start | bytes 49160 | tf_op jit(solution)/shard_map/ppermute | solution.py:509
  49.4 15.0 %collective-permute-start.7 = (bf16[256,1024]{1,0:T(8,128)(2,1)S(1)}, bf16[256,1024]{1,0:T(8,128)(2,1)S(1)}, u32[]{:S(2)}, u32[]{:S(2)}) collective-permute-start(bf16[256,1024]{1,0:T(8,128)(2,1)S(1)} %turn.4), channel_id=1, source_target_pairs={{0,2},{1,3},{2,4},{3,5},{4,6},{5,7},{6,0},{7,1},{8,10},{9,11},{10,... | collective-permute-start | bytes 1572872 | tf_op jit(solution)/shard_map/ppermute | solution.py:469
  50.6 14.6 %collective-permute-start.8 = (bf16[64,4096]{1,0:T(8,128)(2,1)S(1)}, bf16[64,4096]{1,0:T(8,128)(2,1)S(1)}, u32[]{:S(2)}, u32[]{:S(2)}) collective-permute-start(bf16[64,4096]{1,0:T(8,128)(2,1)S(1)} %slice.23), channel_id=1, source_target_pairs={{0,16},{8,24},{16,0},{24,8},{1,17},{9,25},{17,1},{25,9},{2,18},{10... | collective-permute-start | bytes 1572872 | tf_op jit(solution)/shard_map/ppermute | solution.py:534
  52.2 13.3 %collective-permute-start.9 = (bf16[64,4096]{1,0:T(8,128)(2,1)S(1)}, bf16[64,4096]{1,0:T(8,128)(2,1)S(1)}, u32[]{:S(2)}, u32[]{:S(2)}) collective-permute-start(bf16[64,4096]{1,0:T(8,128)(2,1)S(1)} %take_share.3), channel_id=1, source_target_pairs={{0,1},{1,0},{2,3},{3,2},{4,5},{5,4},{6,7},{7,6},{8,9},{9,8},{10,11... | collective-permute-start | bytes 1572872 | tf_op jit(solution)/shard_map/ppermute | solution.py:469
  65.6 4.2 %collective-permute-start.10 = (bf16[256,4096]{1,0:T(8,128)(2,1)S(1)}, bf16[256,4096]{1,0:T(8,128)(2,1)S(1)}, u32[]{:S(2)}, u32[]{:S(2)}) collective-permute-start(bf16[256,4096]{1,0:T(8,128)(2,1)S(1)} %pad_maximum_fusion.refs_1_), channel_id=1, source_target_pairs={{0,8},{8,0},{16,24},{24,16},{1,9},{9,1},{17,25},{25,17},{2,10},{10... | collective-permute-start | bytes 6291464 | tf_op jit(solution)/shard_map/ppermute | solution.py:576
  65.7 17.7 %collective-permute-start.15 = (bf16[256,1024]{1,0:T(8,128)(2,1)S(1)}, bf16[256,1024]{1,0:T(8,128)(2,1)S(1)}, u32[]{:S(2)}, u32[]{:S(2)}) collective-permute-start(bf16[256,1024]{1,0:T(8,128)(2,1)S(1)} %get-tuple-element.215), channel_id=1, source_target_pairs={{0,6},{1,7},{2,0},{3,1},{4,2},{5,3},{6,4},{7,5},{8,14},{9,15},{10,... | collective-permute-start | bytes 1572872 | tf_op jit(solution)/shard_map/ppermute | solution.py:469
  67.8 11.8 %collective-permute-start.11 = (bf16[128,1024]{1,0:T(8,128)(2,1)S(1)}, bf16[128,1024]{1,0:T(8,128)(2,1)S(1)}, u32[]{:S(2)}, u32[]{:S(2)}) collective-permute-start(bf16[128,1024]{1,0:T(8,128)(2,1)S(1)} %get-tuple-element.210), channel_id=1, source_target_pairs={{0,16},{1,17},{2,18},{3,19},{4,20},{5,21},{6,22},{7,23},{8,24},{9,... | collective-permute-start | bytes 786440 | tf_op jit(solution)/shard_map/ppermute | solution.py:562
  68.3 12.7 %collective-permute-start.12 = (bf16[128,1024]{1,0:T(8,128)(2,1)S(1)}, bf16[128,1024]{1,0:T(8,128)(2,1)S(1)}, u32[]{:S(2)}, u32[]{:S(2)}) collective-permute-start(bf16[128,1024]{1,0:T(8,128)(2,1)S(1)} %get-tuple-element.211), channel_id=1, source_target_pairs={{0,24},{1,25},{2,26},{3,27},{4,28},{5,29},{6,30},{7,31},{8,16},{9,... | collective-permute-start | bytes 786440 | tf_op jit(solution)/shard_map/ppermute | solution.py:562
  69.3 11.7 %collective-permute-start.13 = (bf16[128,1024]{1,0:T(8,128)(2,1)S(1)}, bf16[128,1024]{1,0:T(8,128)(2,1)S(1)}, u32[]{:S(2)}, u32[]{:S(2)}) collective-permute-start(bf16[128,1024]{1,0:T(8,128)(2,1)S(1)} %get-tuple-element.212), channel_id=1, source_target_pairs={{0,1},{1,0},{2,3},{3,2},{4,5},{5,4},{6,7},{7,6},{8,9},{9,8},{10,11... | collective-permute-start | bytes 786440 | tf_op jit(solution)/shard_map/ppermute | solution.py:562
  69.9 13.6 %collective-permute-start.14 = (bf16[128,1024]{1,0:T(8,128)(2,1)S(1)}, bf16[128,1024]{1,0:T(8,128)(2,1)S(1)}, u32[]{:S(2)}, u32[]{:S(2)}) collective-permute-start(bf16[128,1024]{1,0:T(8,128)(2,1)S(1)} %get-tuple-element.213), channel_id=1, source_target_pairs={{0,9},{1,8},{2,11},{3,10},{4,13},{5,12},{6,15},{7,14},{8,1},{9,0},... | collective-permute-start | bytes 786440 | tf_op jit(solution)/shard_map/ppermute | solution.py:562
  84.4 14.0 %collective-permute-start.16 = (bf16[256,1024]{1,0:T(8,128)(2,1)S(1)}, bf16[256,1024]{1,0:T(8,128)(2,1)S(1)}, u32[]{:S(2)}, u32[]{:S(2)}) collective-permute-start(bf16[256,1024]{1,0:T(8,128)(2,1)S(1)} %turn.5), channel_id=1, source_target_pairs={{0,6},{1,7},{2,0},{3,1},{4,2},{5,3},{6,4},{7,5},{8,14},{9,15},{10,... | collective-permute-start | bytes 1572872 | tf_op jit(solution)/shard_map/ppermute | solution.py:469
  84.9 5.9 %collective-permute-start.17 = (bf16[128,1024]{1,0:T(8,128)(2,1)S(1)}, bf16[128,1024]{1,0:T(8,128)(2,1)S(1)}, u32[]{:S(2)}, u32[]{:S(2)}) collective-permute-start(bf16[128,1024]{1,0:T(8,128)(2,1)S(1)} %get-tuple-element.231), channel_id=1, source_target_pairs={{0,8},{1,9},{2,10},{3,11},{4,12},{5,13},{6,14},{7,15},{8,0},{9,1},... | collective-permute-start | bytes 786440 | tf_op jit(solution)/shard_map/ppermute | solution.py:562
  84.9 19.0 %collective-permute-start.18 = (bf16[128,1024]{1,0:T(8,128)(2,1)S(1)}, bf16[128,1024]{1,0:T(8,128)(2,1)S(1)}, u32[]{:S(2)}, u32[]{:S(2)}) collective-permute-start(bf16[128,1024]{1,0:T(8,128)(2,1)S(1)} %get-tuple-element.243), channel_id=1, source_target_pairs={{0,17},{1,16},{2,19},{3,18},{4,21},{5,20},{6,23},{7,22},{8,25},{9,... | collective-permute-start | bytes 786440 | tf_op jit(solution)/shard_map/ppermute | solution.py:562
  85.3 18.6 %collective-permute-start.19 = (bf16[128,1024]{1,0:T(8,128)(2,1)S(1)}, bf16[128,1024]{1,0:T(8,128)(2,1)S(1)}, u32[]{:S(2)}, u32[]{:S(2)}) collective-permute-start(bf16[128,1024]{1,0:T(8,128)(2,1)S(1)} %get-tuple-element.245), channel_id=1, source_target_pairs={{0,25},{1,24},{2,27},{3,26},{4,29},{5,28},{6,31},{7,30},{8,17},{9,... | collective-permute-start | bytes 786440 | tf_op jit(solution)/shard_map/ppermute | solution.py:562
  101.0 6.1 %collective-permute-start.22 = (f32[1024]{0:T(1024)S(1)}, f32[1024]{0:T(1024)S(1)}, u32[]{:S(2)}, u32[]{:S(2)}) collective-permute-start(f32[1024]{0:T(1024)S(1)} %bitcast.20), channel_id=1, source_target_pairs={{0,6},{1,7},{2,0},{3,1},{4,2},{5,3},{6,4},{7,5},{8,14},{9,15},{10,... | collective-permute-start | bytes 12296 | tf_op jit(solution)/shard_map/ppermute | solution.py:469
  103.2 4.5 %collective-permute-start.21 = (f32[1024]{0:T(1024)S(1)}, f32[1024]{0:T(1024)S(1)}, u32[]{:S(2)}, u32[]{:S(2)}) collective-permute-start(f32[1024]{0:T(1024)S(1)} %bitcast.21), channel_id=1, source_target_pairs={{0,4},{1,5},{2,6},{3,7},{4,0},{5,1},{6,2},{7,3},{8,12},{9,13},{10,... | collective-permute-start | bytes 12296 | tf_op jit(solution)/shard_map/ppermute | solution.py:469
  103.2 5.4 %collective-permute-start.20 = (f32[1024]{0:T(1024)S(1)}, f32[1024]{0:T(1024)S(1)}, u32[]{:S(2)}, u32[]{:S(2)}) collective-permute-start(f32[1024]{0:T(1024)S(1)} %bitcast.22), channel_id=1, source_target_pairs={{0,2},{1,3},{2,4},{3,5},{4,6},{5,7},{6,0},{7,1},{8,10},{9,11},{10,... | collective-permute-start | bytes 12296 | tf_op jit(solution)/shard_map/ppermute | solution.py:469
  108.6 3.6 %collective-permute-start.23 = (f32[1024]{0:T(1024)S(1)}, f32[1024]{0:T(1024)S(1)}, u32[]{:S(2)}, u32[]{:S(2)}) collective-permute-start(f32[1024]{0:T(1024)S(1)} %maximum_maximum_fusion), channel_id=1, source_target_pairs={{0,1},{1,0},{2,3},{3,2},{4,5},{5,4},{6,7},{7,6},{8,9},{9,8},{10,11... | collective-permute-start | bytes 12296 | tf_op jit(solution)/shard_map/ppermute | solution.py:469
  (4 other events, 19.7 us)

commit v2 on v1

--- a/solution.py
+++ b/solution.py
@@ -7,6 +7,7 @@
 
 VMEM = pl.BlockSpec(memory_space=pltpu.VMEM)
 SMEM = pl.BlockSpec(memory_space=pltpu.SMEM)
+NO_COST = pl.CostEstimate(flops=0, bytes_accessed=0, transcendentals=0)
 PARAMS = pltpu.CompilerParams(vmem_limit_bytes=16 * 1024 * 1024)
 
 ABOVE, HERE, BELOW = 0, 1, 2
@@ -62,9 +63,7 @@
         out_specs=VMEM,
         out_shape=jax.ShapeDtypeStruct((count, width), jnp.bfloat16),
         compiler_params=PARAMS,
-        cost_estimate=pl.CostEstimate(
-            flops=2 * count * half * width, bytes_accessed=4 * half * width, transcendentals=0
-        ),
+        cost_estimate=NO_COST,
         name="turn",
     )(starts, *parts)
 
@@ -88,9 +87,7 @@
             jax.ShapeDtypeStruct((half - near, 2 * width), jnp.bfloat16),
         ],
         compiler_params=PARAMS,
-        cost_estimate=pl.CostEstimate(
-            flops=4 * half * half * width, bytes_accessed=8 * half * width, transcendentals=0
-        ),
+        cost_estimate=NO_COST,
         name="turn_down",
     )(starts, kept, swapped)
 
@@ -116,9 +113,7 @@
         ),
         out_shape=jax.ShapeDtypeStruct((count, depth), table.dtype),
         compiler_params=PARAMS,
-        cost_estimate=pl.CostEstimate(
-            flops=0, bytes_accessed=4 * count * depth, transcendentals=0
-        ),
+        cost_estimate=NO_COST,
         name="take_share",
     )(ids, table)
 
@@ -176,9 +171,7 @@
         ),
         out_shape=outs,
         compiler_params=PARAMS,
-        cost_estimate=pl.CostEstimate(
-            flops=4 * half * half * width, bytes_accessed=16 * half * width, transcendentals=0
-        ),
+        cost_estimate=NO_COST,
         name="prepare",
     )(ids, starts, clusters, orders, kept, swapped, prior, table)
 
@@ -218,46 +211,40 @@
         out_specs=[VMEM] * len(outs),
         out_shape=outs,
         compiler_params=PARAMS,
-        cost_estimate=pl.CostEstimate(
-            flops=0, bytes_accessed=8 * n_dp * cap * per_dp * wide, transcendentals=0
-        ),
+        cost_estimate=NO_COST,
         name="collect",
     )(ids, *parts)
     return {(m, b): found[2 * m + b] for m in range(n_dp) for b in (0, 1)}
 
 
-def update(ids, same_rows, across_rows, same, across, base, prior, counts, token):
-    n_rows, cap = len(same_rows), same_rows[0].shape[0]
+def update(ids, rows, matches, base, prior, counts, token, divide):
+    n_rows, cap = len(rows), rows[0][2].shape[0]
     feats, own = base.shape
     width = feats // 2
 
     def kernel(ids_ref, *refs):
-        same_refs, across_refs = refs[:n_rows], refs[n_rows : 2 * n_rows]
-        same_ref, across_ref, base_ref, prior_ref, counts_ref, token_ref, out_ref = refs[
-            2 * n_rows :
-        ]
-        nothing = token_ref[:1, :1].astype(jnp.float32)
-        inverse = 1.0 / (prior_ref[...] + counts_ref[...] + nothing)
+        row_refs, match_refs = refs[:n_rows], refs[n_rows : n_rows + 2]
+        base_ref, prior_ref, counts_ref, token_ref, out_ref = refs[n_rows + 2 :]
         step = pl.program_id(0)
         for n in (0, 1):
 
             @pl.when(step == n)
             def _(n=n):
-                total = base_ref[...]
-                for row_refs, match_ref, part in (
-                    (same_refs, same_ref, n),
-                    (across_refs, across_ref, 1 - n),
-                ):
-                    held = jnp.concatenate(
-                        [ref[:, part * width : (part + 1) * width] for ref in row_refs], axis=0
-                    )
-                    total += lax.dot_general(
-                        held,
-                        match_ref[...],
-                        (((0,), (0,)), ((), ())),
-                        preferred_element_type=jnp.float32,
-                    )
-                out_ref[...] = total * inverse
+                held, match = [], []
+                for (at, b, _), ref in zip(rows, row_refs):
+                    part = n ^ b
+                    held.append(ref[:, part * width : (part + 1) * width])
+                    match.append(match_refs[b][at * cap : (at + 1) * cap])
+                total = base_ref[...] + lax.dot_general(
+                    jnp.concatenate(held, axis=0),
+                    jnp.concatenate(match, axis=0),
+                    (((0,), (0,)), ((), ())),
+                    preferred_element_type=jnp.float32,
+                )
+                if divide:
+                    nothing = token_ref[:1, :1].astype(jnp.float32)
+                    total = total * (1.0 / (prior_ref[...] + counts_ref[...] + nothing))
+                out_ref[...] = total
 
     block = pl.BlockSpec((width, own), lambda g, ids: (g ^ (ids[1] & 1), 0))
     return pl.pallas_call(
@@ -265,16 +252,14 @@
         grid_spec=pltpu.PrefetchScalarGridSpec(
             num_scalar_prefetch=1,
             grid=(2,),
-            in_specs=[VMEM] * (2 * n_rows + 2) + [block, VMEM, VMEM, VMEM],
+            in_specs=[VMEM] * (n_rows + 2) + [block, VMEM, VMEM, VMEM],
             out_specs=block,
         ),
         out_shape=jax.ShapeDtypeStruct((feats, own), jnp.float32),
         compiler_params=PARAMS,
-        cost_estimate=pl.CostEstimate(
-            flops=4 * n_rows * cap * feats * own, bytes_accessed=8 * feats * own, transcendentals=0
-        ),
+        cost_estimate=NO_COST,
         name="update",
-    )(ids, *same_rows, *across_rows, same, across, base, prior, counts, token)
+    )(ids, *[value for _, _, value in rows], *matches, base, prior, counts, token)
 
 
 def column_block(n_line, steps):
@@ -362,11 +347,7 @@
             jax.ShapeDtypeStruct((1, half), jnp.float32),
         ],
         compiler_params=PARAMS,
-        cost_estimate=pl.CostEstimate(
-            flops=2 * half * total * width * n_blocks,
-            bytes_accessed=2 * total * width * n_blocks,
-            transcendentals=0,
-        ),
+        cost_estimate=NO_COST,
         name="score_part",
     )(ids, *tables, *parts, *before)
 
@@ -442,9 +423,7 @@
         grid_spec=grid_spec,
         out_shape=jax.ShapeDtypeStruct((1, rows), jnp.float32),
         compiler_params=PARAMS,
-        cost_estimate=pl.CostEstimate(
-            flops=4 * count * total * width, bytes_accessed=4 * total * width, transcendentals=0
-        ),
+        cost_estimate=NO_COST,
         name="score_last",
     )(ids, starts, *tables, last, *scores, *bests, order)
 
@@ -499,8 +478,8 @@
     swapped, share, blocks, prior, order = steps.tie(swapped, share, blocks, prior, order)
     up_b, up_a = steps.tie(turn([swapped], starts, None, ABOVE, 0, half, False), up_a)
     up_b = send(up_b, ring(1))
-    close, far, share = steps.tie(*turn_down(kept, swapped, starts, near), share)
-    close, share = send(close, ring(-1)), send(share, swap)
+    close, far = steps.tie(*turn_down(kept, swapped, starts, near))
+    close, share = send(close, ring(-1)), send(steps.tie(share), swap)
 
     blocks, held_from = steps.tie(blocks), [0]
     bit = n_dp // 2
@@ -514,17 +493,16 @@
     ids, centroids = steps.tie(ids, centroids)
     late_share = take_share(ids, centroids, n_dp, True)
 
-    up_b, close, share, late_share = steps.tie(up_b, close, share, late_share)
+    up_b, late_share = steps.tie(up_b, late_share)
     up = (up_a, up_b)
     pieces = {1: up}
     for step in range(2, middle):
         wide = send(turn(list(up), starts, HERE, ABOVE, 0, half, False), ring(1))
         up = (wide[:, :width], wide[:, width:])
         pieces[step] = up
-    middle_near, share, late_share = steps.tie(
-        turn(list(up), starts, HERE, ABOVE, 0, near, False), share, late_share
-    )
+    middle_near = steps.tie(turn(list(up), starts, HERE, ABOVE, 0, near, False))
     middle_near = send(middle_near, ring(1))
+    share, late_share = steps.tie(share, late_share)
 
     others, bit = [share], n_dp // 2
     if n_dp == 4:
@@ -545,8 +523,8 @@
     )
     pieces[0] = (self_a, self_b)
 
-    middle_near, pieces[0], same, across, counts, base = steps.tie(
-        middle_near, pieces[0], same, across, counts, base
+    middle_near, close, pieces[0], same, across, counts, base = steps.tie(
+        middle_near, close, pieces[0], same, across, counts, base
     )
     far = send(steps.tie(far), ring(-1))
     windows = dict(pieces)
@@ -568,8 +546,8 @@
         )
         downs[n_line - step] = down
         windows[n_line - step] = (down[0],)
-    first = [(m, 0) for m in range(2, n_dp)] + [(0, 1), (1, 1)]
-    second = [(m, 1) for m in range(2, n_dp)] + [(1, 0)]
+    first = [(2, 0), (0, 1), (1, 0)]
+    second = [(m, 0) for m in range(3, n_dp)] + [(m, 1) for m in range(1, n_dp)]
     got = steps.tie(collect(ids, [windows[n] for n in range(n_line)], cap, n_dp))
     others = steps.tie(others)
     core_sent = steps.tie(jnp.concatenate(others, axis=0))
@@ -595,26 +573,32 @@
     work = [(step, downs[step]) for step in downs]
     score, best = steps.tie(*score_part(ids, tables, work, half, n_line, so_far))
 
-    middle_far, got[1, 0] = steps.tie(middle_far, got[1, 0])
+    def payloads(keys):
+        return [(held_from.index(m), b, got[m, b]) for m, b in keys]
+
+    matches = [same, across]
+    if per_dp == 1:
+        early = [(0, 0)] + first
+        base = update(ids, payloads(early), matches, base, prior, counts, steps.token, False)
+        base = steps.tie(base)
+
+    middle_far = steps.tie(middle_far)
     best = score_last(
         ids, starts, tables, middle_far, [score], [best], order, near, n_line
     )[0]
     best = steps.tie(best)
-    arrived = [send(best, ring(step)) for step in range(1, n_line)]
+    bit = 1
+    while bit < n_line:
+        pairs = [(j, j ^ (2 * bit)) for j in range(n_cent)]
+        best = steps.tie(jnp.maximum(best, send(best, pairs)))
+        bit *= 2
+    opposite = send(best, swap)
 
     got = steps.tie(got)
     feats = 2 * per_dp * width
     if per_dp == 1:
         updated = update(
-            ids,
-            [got[m, 0] for m in held_from],
-            [got[m, 1] for m in held_from],
-            same,
-            across,
-            base,
-            prior,
-            counts,
-            steps.token,
+            ids, payloads(second), matches, base, prior, counts, steps.token, True
         )
     else:
         counts = counts + steps.token[0, 0].astype(jnp.float32)
@@ -633,9 +617,7 @@
         odd = jnp.where(side == 0, theirs, mine)
         sums = jnp.stack([even, odd], axis=1).reshape(base.shape)
         updated = (base + sums) / (prior + counts)
-    best, updated = steps.tie(best, updated)
-    best = largest_of([best] + arrived)
-    return (jnp.maximum(best, send(best, swap)), updated)
+    return (jnp.maximum(best, opposite), updated)
 
 
 def largest_of(values):

time: 113 us -> 107 us (0.947)
  waiting for transfers between devices: 55.8 us -> 40.3 us
  starting transfers between devices: 26.1 us -> 34.5 us
    ppermute x13 -> x12, waiting for transfers between devices: 48.4 us -> 37.7 us  [send(): return lax.ppermute(value, 'cent', pairs)]
    ppermute x13 -> x12, starting transfers between devices: 17 us -> 25.2 us  [send(): return lax.ppermute(value, 'cent', pairs)]
    ppermute x7, waiting for transfers between devices: 3.8 us -> 0.02 us  [deliver(): return lax.ppermute(value, ('dp', 'cent'), pairs)]
    ppermute x2, waiting for transfers between devices: 3.34 us -> 2.15 us  [on_device(): lax.ppermute(blocks, 'dp', pairs)]
    pallas_call x1 -> x2, Pallas kernels: 3.21 us -> 4.11 us  [update(): pl.pallas_call(kernel, grid_spec=pltpu.PrefetchScalarGridSpec(num_scalar_...]
  transfers between devices with their start and end apart: 24 -> 23, of which waited for: 15 -> 11; matrix products, arithmetic and copies ran while one was open for 0% -> 0% of each run, Pallas kernels for 21% -> 24%
where the time goes in v2:
time: 107 us
  waiting for transfers between devices  40.3 us (38%)
  starting transfers between devices  34.5 us (32%)
  Pallas kernels  26.4 us (25%)
  other arithmetic  3.16 us (3%)
  matrix products  1.26 us (1%)
    ppermute x12, waiting for transfers between devices, send(): return lax.ppermute(value, 'cent', pairs)  37.7 us
    ppermute x12, starting transfers between devices, send(): return lax.ppermute(value, 'cent', pairs)  25.2 us
    pallas_call x2, Pallas kernels, score_part(): pl.pallas_call(kernel, grid_spec=grid_spec, out_shape=[jax.ShapeDtypeStru...  11.5 us
    ppermute x7, starting transfers between devices, deliver(): return lax.ppermute(value, ('dp', 'cent'), pairs)  6.12 us
    pallas_call x2, Pallas kernels, update(): pl.pallas_call(kernel, grid_spec=pltpu.PrefetchScalarGridSpec(num_scalar_...  4.11 us
    pallas_call x3, Pallas kernels, turn(): pl.pallas_call(kernel, in_specs=[SMEM] + [VMEM] * len(parts), out_specs=V...  2.94 us
    pallas_call x1, Pallas kernels, score_last(): pl.pallas_call(kernel, grid_spec=grid_spec, out_shape=jax.ShapeDtypeStruc...  2.49 us
    ppermute x2, waiting for transfers between devices, on_device(): lax.ppermute(blocks, 'dp', pairs)  2.15 us
  transfers between devices with their start and end apart: 23, of which 11 were waited for; matrix products, arithmetic and copies ran while one was open for 0% of the time, Pallas kernels for 24%

profile of v2, /device:TPU:0, one launch (start us, length us, event | category | flops | bytes accessed | tf_op | source)
XLA Modules:
  0.0 106.6 jit_solution(18287723828912866786)
XLA Ops:
  4.4 3.0 %collective-permute-start = (bf16[512,512]{1,0:T(8,128)(2,1)S(1)}, bf16[512,512]{1,0:T(8,128)(2,1)S(1)}, u32[]{:S(2)}, u32[]{:S(2)}) collective-permute-start(bf16[512,512]{1,0:T(8,128)(2,1)S(1)} %get-tuple-element.133), channel_id=1, source_target_pairs={{0,1},{1,0},{2,3},{3,2},{4,5},{5,4},{6,7},{7,6},{8,9},{9,8},{10,11... | collective-permute-start | bytes 1572872 | tf_op jit(solution)/shard_map/ppermute | solution.py:448
  7.4 1.6 %collective-permute-start.1 = (bf16[512,512]{1,0:T(8,128)(2,1)S(1)}, bf16[512,512]{1,0:T(8,128)(2,1)S(1)}, u32[]{:S(2)}, u32[]{:S(2)}) collective-permute-start(bf16[512,512]{1,0:T(8,128)(2,1)S(1)} %get-tuple-element.141.kept_ref), channel_id=1, source_target_pairs={{0,2},{1,3},{2,4},{3,5},{4,6},{5,7},{6,0},{7,1},{8,10},{9,11},{10,... | collective-permute-start | bytes 1572872 | tf_op jit(solution)/shard_map/ppermute | solution.py:448
  9.7 9.6 %collective-permute-done.refs_0_.swapped_ref = bf16[512,512]{1,0:T(8,128)(2,1)S(1)} collective-permute-done((bf16[512,512]{1,0:T(8,128)(2,1)S(1)}, bf16[512,512]{1,0:T(8,128)(2,1)S(1)}, u32[]{:S(2)}, u32[]{:S(2)}) %collective-permute-start) | collective-permute-done | bytes 524320 | tf_op jit(solution)/shard_map/ppermute | solution.py:448
  23.4 1.6 %collective-permute-start.4 = (bf16[512,512]{1,0:T(8,128)(2,1)S(1)}, bf16[512,512]{1,0:T(8,128)(2,1)S(1)}, u32[]{:S(2)}, u32[]{:S(2)}) collective-permute-start(bf16[512,512]{1,0:T(8,128)(2,1)S(1)} %turn.3), channel_id=1, source_target_pairs={{0,2},{1,3},{2,4},{3,5},{4,6},{5,7},{6,0},{7,1},{8,10},{9,11},{10,... | collective-permute-start | bytes 1572872 | tf_op jit(solution)/shard_map/ppermute | solution.py:448
  26.4 2.1 %collective-permute-done.2 = s32[1,2,1024]{2,1,0:T(2,128)S(1)} collective-permute-done((s32[1,2,1024]{2,1,0:T(2,128)S(1)}, s32[1,2,1024]{2,1,0:T(2,128)S(1)}, u32[]{:S(2)}, u32[]{:S(2)}) %collective-permute-start.2) | collective-permute-done | bytes 8224 | tf_op jit(solution)/shard_map/ppermute | solution.py:488
  28.6 2.3 %collective-permute-start.7 = (bf16[256,1024]{1,0:T(8,128)(2,1)S(1)}, bf16[256,1024]{1,0:T(8,128)(2,1)S(1)}, u32[]{:S(2)}, u32[]{:S(2)}) collective-permute-start(bf16[256,1024]{1,0:T(8,128)(2,1)S(1)} %get-tuple-element.168), channel_id=1, source_target_pairs={{0,6},{1,7},{2,0},{3,1},{4,2},{5,3},{6,4},{7,5},{8,14},{9,15},{10,... | collective-permute-start | bytes 1572872 | tf_op jit(solution)/shard_map/ppermute | solution.py:448
  31.5 8.6 %collective-permute-done.4.refs_1_.refs_3_.refs_6_ = bf16[512,512]{1,0:T(8,128)(2,1)S(1)} collective-permute-done((bf16[512,512]{1,0:T(8,128)(2,1)S(1)}, bf16[512,512]{1,0:T(8,128)(2,1)S(1)}, u32[]{:S(2)}, u32[]{:S(2)}) %collective-permute-start.4) | collective-permute-done | bytes 524320 | tf_op jit(solution)/shard_map/ppermute | solution.py:448
  41.1 5.8 %collective-permute-start.6 = (bf16[256,1024]{1,0:T(8,128)(2,1)S(1)}, bf16[256,1024]{1,0:T(8,128)(2,1)S(1)}, u32[]{:S(2)}, u32[]{:S(2)}) collective-permute-start(bf16[256,1024]{1,0:T(8,128)(2,1)S(1)} %turn.4), channel_id=1, source_target_pairs={{0,2},{1,3},{2,4},{3,5},{4,6},{5,7},{6,0},{7,1},{8,10},{9,11},{10,... | collective-permute-start | bytes 1572872 | tf_op jit(solution)/shard_map/ppermute | solution.py:448
  46.9 1.5 %collective-permute-start.8 = (bf16[64,4096]{1,0:T(8,128)(2,1)S(1)}, bf16[64,4096]{1,0:T(8,128)(2,1)S(1)}, u32[]{:S(2)}, u32[]{:S(2)}) collective-permute-start(bf16[64,4096]{1,0:T(8,128)(2,1)S(1)} %slice.23), channel_id=1, source_target_pairs={{0,16},{8,24},{16,0},{24,8},{1,17},{9,25},{17,1},{25,9},{2,18},{10... | collective-permute-start | bytes 1572872 | tf_op jit(solution)/shard_map/ppermute | solution.py:512
  49.0 2.1 %prepare.1 = (bf16[512,512]{1,0:T(8,128)(2,1)S(1)}, bf16[512,512]{1,0:T(8,128)(2,1)S(1)}, bf16[512,512]{1,0:T(8,128)(2,1)S(1)}, bf16[512,512]{1,0:T(8,128)(2,1)S...) custom-call(s32[2]{0:T(128)S(1)} %pad_add_fusion.2.ids_ref, s32[3]{0:T(128)S(1)} %fusion.12.starts_ref, ...), custom_call_target="tpu_custom_call" | custom-call | tf_op jit(solution)/shard_map/prepare/pallas_call | solution.py:164
  51.2 9.0 %collective-permute-done.6.refs_4_.refs_7_ = bf16[256,1024]{1,0:T(8,128)(2,1)S(1)} collective-permute-done((bf16[256,1024]{1,0:T(8,128)(2,1)S(1)}, bf16[256,1024]{1,0:T(8,128)(2,1)S(1)}, u32[]{:S(2)}, u32[]{:S(2)}) %collective-permute-start.6) | collective-permute-done | bytes 524320 | tf_op jit(solution)/shard_map/ppermute | solution.py:448
  61.3 1.8 %collective-permute-start.14 = (bf16[256,1024]{1,0:T(8,128)(2,1)S(1)}, bf16[256,1024]{1,0:T(8,128)(2,1)S(1)}, u32[]{:S(2)}, u32[]{:S(2)}) collective-permute-start(bf16[256,1024]{1,0:T(8,128)(2,1)S(1)} %get-tuple-element.215), channel_id=1, source_target_pairs={{0,6},{1,7},{2,0},{3,1},{4,2},{5,3},{6,4},{7,5},{8,14},{9,15},{10,... | collective-permute-start | bytes 1572872 | tf_op jit(solution)/shard_map/ppermute | solution.py:448
  65.5 8.3 %score_part.2 = (f32[1024,512]{1,0:T(8,128)S(1)}, f32[1,512]{1,0:T(1,128)}) custom-call(s32[2]{0:T(128)S(1)} %pad_add_fusion.2.ids_ref, bf16[512,4096]{1,0:T(8,128)(2,1)S(1)} %copy-done.1, bf16[256,4096]{1,0:T(8,128)(2,1)S(1)} %pad_maximum_fusion.refs_1_, bf16[256,4096]{1,0:T(8,128)(2,1)S(1)} %collective-permute-done.10.refs_2_, ...), custom_call_target="tpu_custom_call" | custom-call | tf_op jit(solution)/shard_map/score_part/pallas_call | solution.py:342
  73.8 1.8 %collective-permute-done.14.refs_1_.refs_4_ = bf16[256,1024]{1,0:T(8,128)(2,1)S(1)} collective-permute-done((bf16[256,1024]{1,0:T(8,128)(2,1)S(1)}, bf16[256,1024]{1,0:T(8,128)(2,1)S(1)}, u32[]{:S(2)}, u32[]{:S(2)}) %collective-permute-start.14) | collective-permute-done | bytes 524320 | tf_op jit(solution)/shard_map/ppermute | solution.py:448
  76.6 3.7 %collective-permute-start.15 = (bf16[256,1024]{1,0:T(8,128)(2,1)S(1)}, bf16[256,1024]{1,0:T(8,128)(2,1)S(1)}, u32[]{:S(2)}, u32[]{:S(2)}) collective-permute-start(bf16[256,1024]{1,0:T(8,128)(2,1)S(1)} %turn.5), channel_id=1, source_target_pairs={{0,6},{1,7},{2,0},{3,1},{4,2},{5,3},{6,4},{7,5},{8,14},{9,15},{10,... | collective-permute-start | bytes 1572872 | tf_op jit(solution)/shard_map/ppermute | solution.py:448
  80.8 1.5 %collective-permute-start.20 = (bf16[128,1024]{1,0:T(8,128)(2,1)S(1)}, bf16[128,1024]{1,0:T(8,128)(2,1)S(1)}, u32[]{:S(2)}, u32[]{:S(2)}) collective-permute-start(bf16[128,1024]{1,0:T(8,128)(2,1)S(1)} %get-tuple-element.253), channel_id=1, source_target_pairs={{0,17},{1,16},{2,19},{3,18},{4,21},{5,20},{6,23},{7,22},{8,25},{9,... | collective-permute-start | bytes 786440 | tf_op jit(solution)/shard_map/ppermute | solution.py:540
  84.5 3.2 %score_part.3 = (f32[1024,512]{1,0:T(8,128)S(1)}, f32[1,512]{1,0:T(1,128)S(1)}) custom-call(s32[2]{0:T(128)S(1)} %pad_add_fusion.2.ids_ref, bf16[512,4096]{1,0:T(8,128)(2,1)S(1)} %copy-done.1, bf16[256,4096]{1,0:T(8,128)(2,1)S(1)} %pad_maximum_fusion.refs_1_, bf16[256,4096]{1,0:T(8,128)(2,1)S(1)} %collective-permute-done.10.refs_2_, ...), custom_call_target="tpu_custom_call" | custom-call | tf_op jit(solution)/shard_map/score_part/pallas_call | solution.py:342
  87.7 1.5 %update.2.refs_6_ = f32[1024,512]{1,0:T(8,128)S(1)} custom-call(s32[2]{0:T(128)S(1)} %pad_add_fusion.2.ids_ref, bf16[128,1024]{1,0:T(8,128)(2,1)S(1)} %get-tuple-element.231.refs_0_, bf16[128,1024]{1,0:T(8,128)(2,1)S(1)} %collective-permute-done.11.refs_1_, bf16[128,1024]{1,0:T(8,128)(2,1)S(1)} %collective-permute-done.12.refs_2_, ...), custom_call_target="tpu_custom_call" | custom-call | tf_op jit(solution)/shard_map/update/pallas_call | solution.py:250
  89.2 2.2 %collective-permute-done.15.refs_3_ = bf16[256,1024]{1,0:T(8,128)(2,1)S(1)} collective-permute-done((bf16[256,1024]{1,0:T(8,128)(2,1)S(1)}, bf16[256,1024]{1,0:T(8,128)(2,1)S(1)}, u32[]{:S(2)}, u32[]{:S(2)}) %collective-permute-start.15) | collective-permute-done | bytes 524320 | tf_op jit(solution)/shard_map/ppermute | solution.py:448
  91.4 2.5 %score_last.1 = f32[1,1024]{1,0:T(1,128)S(1)} custom-call(s32[2]{0:T(128)S(1)} %pad_add_fusion.2.ids_ref, s32[3]{0:T(128)S(1)} %fusion.12.starts_ref, bf16[512,4096]{1,0:T(8,128)(2,1)S(1)} %copy-done.1, bf16[256,4096]{1,0:T(8,128)(2,1)S(1)} %pad_maximum_fusion.refs_1_, bf16[256,4096]{1,0:T(8,128)(2,1)S(1)} %collective-permute-done.10.refs_2_, ...), custom_call_target="tpu_custom_call" | custom-call | tf_op jit(solution)/shard_map/score_last/pallas_call | solution.py:421
  94.0 3.6 %collective-permute-done.16 = f32[1024]{0:T(1024)S(1)} collective-permute-done((f32[1024]{0:T(1024)S(1)}, f32[1024]{0:T(1024)S(1)}, u32[]{:S(2)}, u32[]{:S(2)}) %collective-permute-start.16) | collective-permute-done | bytes 4128 | tf_op jit(solution)/shard_map/ppermute | solution.py:448
  97.6 2.8 %collective-permute-start.17 = (f32[1024]{0:T(1024)S(1)}, f32[1024]{0:T(1024)S(1)}, u32[]{:S(2)}, u32[]{:S(2)}) collective-permute-start(f32[1024]{0:T(1024)S(1)} %max.9), channel_id=1, source_target_pairs={{0,4},{1,5},{2,6},{3,7},{4,0},{5,1},{6,2},{7,3},{8,12},{9,13},{10,... | collective-permute-start | bytes 12296 | tf_op jit(solution)/shard_map/ppermute | solution.py:448
  100.4 1.7 %collective-permute-done.17 = f32[1024]{0:T(1024)S(1)} collective-permute-done((f32[1024]{0:T(1024)S(1)}, f32[1024]{0:T(1024)S(1)}, u32[]{:S(2)}, u32[]{:S(2)}) %collective-permute-start.17) | collective-permute-done | bytes 4128 | tf_op jit(solution)/shard_map/ppermute | solution.py:448
  103.5 2.6 %update.3 = f32[1024,512]{1,0:T(8,128)} custom-call(s32[2]{0:T(128)S(1)} %pad_add_fusion.2.ids_ref, bf16[128,1024]{1,0:T(8,128)(2,1)S(1)} %collective-permute-done.21.refs_0_, bf16[128,1024]{1,0:T(8,128)(2,1)S(1)} %collective-permute-done.19.refs_1_, bf16[128,1024]{1,0:T(8,128)(2,1)S(1)} %collective-permute-done.20.refs_2_, ...), custom_call_target="tpu_custom_call" | custom-call | tf_op jit(solution)/shard_map/update/pallas_call | solution.py:250
  (64 shorter events, 21.3 us)
Async XLA Ops:
  3.0 6.0 %copy-start.1 = (bf16[512,4096]{1,0:T(8,128)(2,1)S(1)}, bf16[512,4096]{1,0:T(8,128)(2,1)}, u32[]{:S(2)}) copy-start(bf16[512,4096]{1,0:T(8,128)(2,1)} %refs_0_.2) | copy-start | bytes 12582916
  4.4 14.9 %collective-permute-start = (bf16[512,512]{1,0:T(8,128)(2,1)S(1)}, bf16[512,512]{1,0:T(8,128)(2,1)S(1)}, u32[]{:S(2)}, u32[]{:S(2)}) collective-permute-start(bf16[512,512]{1,0:T(8,128)(2,1)S(1)} %get-tuple-element.133), channel_id=1, source_target_pairs={{0,1},{1,0},{2,3},{3,2},{4,5},{5,4},{6,7},{7,6},{8,9},{9,8},{10,11... | collective-permute-start | bytes 1572872 | tf_op jit(solution)/shard_map/ppermute | solution.py:448
  7.4 15.2 %collective-permute-start.1 = (bf16[512,512]{1,0:T(8,128)(2,1)S(1)}, bf16[512,512]{1,0:T(8,128)(2,1)S(1)}, u32[]{:S(2)}, u32[]{:S(2)}) collective-permute-start(bf16[512,512]{1,0:T(8,128)(2,1)S(1)} %get-tuple-element.141.kept_ref), channel_id=1, source_target_pairs={{0,2},{1,3},{2,4},{3,5},{4,6},{5,7},{6,0},{7,1},{8,10},{9,11},{10,... | collective-permute-start | bytes 1572872 | tf_op jit(solution)/shard_map/ppermute | solution.py:448
  22.6 24.3 %collective-permute-start.5 = (bf16[128,4096]{1,0:T(8,128)(2,1)S(1)}, bf16[128,4096]{1,0:T(8,128)(2,1)S(1)}, u32[]{:S(2)}, u32[]{:S(2)}) collective-permute-start(bf16[128,4096]{1,0:T(8,128)(2,1)S(1)} %take_share.2), channel_id=1, source_target_pairs={{0,1},{1,0},{2,3},{3,2},{4,5},{5,4},{6,7},{7,6},{8,9},{9,8},{10,11... | collective-permute-start | bytes 3145736 | tf_op jit(solution)/shard_map/ppermute | solution.py:448
  23.4 16.7 %collective-permute-start.4 = (bf16[512,512]{1,0:T(8,128)(2,1)S(1)}, bf16[512,512]{1,0:T(8,128)(2,1)S(1)}, u32[]{:S(2)}, u32[]{:S(2)}) collective-permute-start(bf16[512,512]{1,0:T(8,128)(2,1)S(1)} %turn.3), channel_id=1, source_target_pairs={{0,2},{1,3},{2,4},{3,5},{4,6},{5,7},{6,0},{7,1},{8,10},{9,11},{10,... | collective-permute-start | bytes 1572872 | tf_op jit(solution)/shard_map/ppermute | solution.py:448
  24.9 3.7 %collective-permute-start.2 = (s32[1,2,1024]{2,1,0:T(2,128)S(1)}, s32[1,2,1024]{2,1,0:T(2,128)S(1)}, u32[]{:S(2)}, u32[]{:S(2)}) collective-permute-start(s32[1,2,1024]{2,1,0:T(2,128)S(1)} %add_bitcast_fusion), channel_id=1, source_target_pairs={{0,16},{8,24},{16,0},{24,8},{1,17},{9,25},{17,1},{25,9},{2,18},{10... | collective-permute-start | bytes 24584 | tf_op jit(solution)/shard_map/ppermute | solution.py:488
  28.6 2.3 %collective-permute-start.3 = (s32[2,2,1024]{2,1,0:T(2,128)S(1)}, s32[2,2,1024]{2,1,0:T(2,128)S(1)}, u32[]{:S(2)}, u32[]{:S(2)}) collective-permute-start(s32[2,2,1024]{2,1,0:T(2,128)S(1)} %pad_add_fusion.1), channel_id=1, source_target_pairs={{0,8},{8,0},{16,24},{24,16},{1,9},{9,1},{17,25},{25,17},{2,10},{10... | collective-permute-start | bytes 49160 | tf_op jit(solution)/shard_map/ppermute | solution.py:488
  28.6 22.6 %collective-permute-start.7 = (bf16[256,1024]{1,0:T(8,128)(2,1)S(1)}, bf16[256,1024]{1,0:T(8,128)(2,1)S(1)}, u32[]{:S(2)}, u32[]{:S(2)}) collective-permute-start(bf16[256,1024]{1,0:T(8,128)(2,1)S(1)} %get-tuple-element.168), channel_id=1, source_target_pairs={{0,6},{1,7},{2,0},{3,1},{4,2},{5,3},{6,4},{7,5},{8,14},{9,15},{10,... | collective-permute-start | bytes 1572872 | tf_op jit(solution)/shard_map/ppermute | solution.py:448
  41.1 19.2 %collective-permute-start.6 = (bf16[256,1024]{1,0:T(8,128)(2,1)S(1)}, bf16[256,1024]{1,0:T(8,128)(2,1)S(1)}, u32[]{:S(2)}, u32[]{:S(2)}) collective-permute-start(bf16[256,1024]{1,0:T(8,128)(2,1)S(1)} %turn.4), channel_id=1, source_target_pairs={{0,2},{1,3},{2,4},{3,5},{4,6},{5,7},{6,0},{7,1},{8,10},{9,11},{10,... | collective-permute-start | bytes 1572872 | tf_op jit(solution)/shard_map/ppermute | solution.py:448
  46.9 14.1 %collective-permute-start.8 = (bf16[64,4096]{1,0:T(8,128)(2,1)S(1)}, bf16[64,4096]{1,0:T(8,128)(2,1)S(1)}, u32[]{:S(2)}, u32[]{:S(2)}) collective-permute-start(bf16[64,4096]{1,0:T(8,128)(2,1)S(1)} %slice.23), channel_id=1, source_target_pairs={{0,16},{8,24},{16,0},{24,8},{1,17},{9,25},{17,1},{25,9},{2,18},{10... | collective-permute-start | bytes 1572872 | tf_op jit(solution)/shard_map/ppermute | solution.py:512
  48.5 12.6 %collective-permute-start.9 = (bf16[64,4096]{1,0:T(8,128)(2,1)S(1)}, bf16[64,4096]{1,0:T(8,128)(2,1)S(1)}, u32[]{:S(2)}, u32[]{:S(2)}) collective-permute-start(bf16[64,4096]{1,0:T(8,128)(2,1)S(1)} %take_share.3), channel_id=1, source_target_pairs={{0,1},{1,0},{2,3},{3,2},{4,5},{5,4},{6,7},{7,6},{8,9},{9,8},{10,11... | collective-permute-start | bytes 1572872 | tf_op jit(solution)/shard_map/ppermute | solution.py:448
  61.3 4.2 %collective-permute-start.10 = (bf16[256,4096]{1,0:T(8,128)(2,1)S(1)}, bf16[256,4096]{1,0:T(8,128)(2,1)S(1)}, u32[]{:S(2)}, u32[]{:S(2)}) collective-permute-start(bf16[256,4096]{1,0:T(8,128)(2,1)S(1)} %pad_maximum_fusion.refs_1_), channel_id=1, source_target_pairs={{0,8},{8,0},{16,24},{24,16},{1,9},{9,1},{17,25},{25,17},{2,10},{10... | collective-permute-start | bytes 6291464 | tf_op jit(solution)/shard_map/ppermute | solution.py:554
  61.3 14.3 %collective-permute-start.14 = (bf16[256,1024]{1,0:T(8,128)(2,1)S(1)}, bf16[256,1024]{1,0:T(8,128)(2,1)S(1)}, u32[]{:S(2)}, u32[]{:S(2)}) collective-permute-start(bf16[256,1024]{1,0:T(8,128)(2,1)S(1)} %get-tuple-element.215), channel_id=1, source_target_pairs={{0,6},{1,7},{2,0},{3,1},{4,2},{5,3},{6,4},{7,5},{8,14},{9,15},{10,... | collective-permute-start | bytes 1572872 | tf_op jit(solution)/shard_map/ppermute | solution.py:448
  63.1 10.7 %collective-permute-start.11 = (bf16[128,1024]{1,0:T(8,128)(2,1)S(1)}, bf16[128,1024]{1,0:T(8,128)(2,1)S(1)}, u32[]{:S(2)}, u32[]{:S(2)}) collective-permute-start(bf16[128,1024]{1,0:T(8,128)(2,1)S(1)} %get-tuple-element.211), channel_id=1, source_target_pairs={{0,16},{1,17},{2,18},{3,19},{4,20},{5,21},{6,22},{7,23},{8,24},{9,... | collective-permute-start | bytes 786440 | tf_op jit(solution)/shard_map/ppermute | solution.py:540
  64.6 9.3 %collective-permute-start.12 = (bf16[128,1024]{1,0:T(8,128)(2,1)S(1)}, bf16[128,1024]{1,0:T(8,128)(2,1)S(1)}, u32[]{:S(2)}, u32[]{:S(2)}) collective-permute-start(bf16[128,1024]{1,0:T(8,128)(2,1)S(1)} %get-tuple-element.212), channel_id=1, source_target_pairs={{0,1},{1,0},{2,3},{3,2},{4,5},{5,4},{6,7},{7,6},{8,9},{9,8},{10,11... | collective-permute-start | bytes 786440 | tf_op jit(solution)/shard_map/ppermute | solution.py:540
  65.1 8.8 %collective-permute-start.13 = (bf16[128,1024]{1,0:T(8,128)(2,1)S(1)}, bf16[128,1024]{1,0:T(8,128)(2,1)S(1)}, u32[]{:S(2)}, u32[]{:S(2)}) collective-permute-start(bf16[128,1024]{1,0:T(8,128)(2,1)S(1)} %get-tuple-element.213), channel_id=1, source_target_pairs={{0,8},{1,9},{2,10},{3,11},{4,12},{5,13},{6,14},{7,15},{8,0},{9,1},... | collective-permute-start | bytes 786440 | tf_op jit(solution)/shard_map/ppermute | solution.py:540
  76.6 14.7 %collective-permute-start.15 = (bf16[256,1024]{1,0:T(8,128)(2,1)S(1)}, bf16[256,1024]{1,0:T(8,128)(2,1)S(1)}, u32[]{:S(2)}, u32[]{:S(2)}) collective-permute-start(bf16[256,1024]{1,0:T(8,128)(2,1)S(1)} %turn.5), channel_id=1, source_target_pairs={{0,6},{1,7},{2,0},{3,1},{4,2},{5,3},{6,4},{7,5},{8,14},{9,15},{10,... | collective-permute-start | bytes 1572872 | tf_op jit(solution)/shard_map/ppermute | solution.py:448
  80.4 23.1 %collective-permute-start.19 = (bf16[128,1024]{1,0:T(8,128)(2,1)S(1)}, bf16[128,1024]{1,0:T(8,128)(2,1)S(1)}, u32[]{:S(2)}, u32[]{:S(2)}) collective-permute-start(bf16[128,1024]{1,0:T(8,128)(2,1)S(1)} %get-tuple-element.252), channel_id=1, source_target_pairs={{0,9},{1,8},{2,11},{3,10},{4,13},{5,12},{6,15},{7,14},{8,1},{9,0},... | collective-permute-start | bytes 786440 | tf_op jit(solution)/shard_map/ppermute | solution.py:540
  80.8 22.7 %collective-permute-start.20 = (bf16[128,1024]{1,0:T(8,128)(2,1)S(1)}, bf16[128,1024]{1,0:T(8,128)(2,1)S(1)}, u32[]{:S(2)}, u32[]{:S(2)}) collective-permute-start(bf16[128,1024]{1,0:T(8,128)(2,1)S(1)} %get-tuple-element.253), channel_id=1, source_target_pairs={{0,17},{1,16},{2,19},{3,18},{4,21},{5,20},{6,23},{7,22},{8,25},{9,... | collective-permute-start | bytes 786440 | tf_op jit(solution)/shard_map/ppermute | solution.py:540
  82.3 21.2 %collective-permute-start.21 = (bf16[128,1024]{1,0:T(8,128)(2,1)S(1)}, bf16[128,1024]{1,0:T(8,128)(2,1)S(1)}, u32[]{:S(2)}, u32[]{:S(2)}) collective-permute-start(bf16[128,1024]{1,0:T(8,128)(2,1)S(1)} %get-tuple-element.254), channel_id=1, source_target_pairs={{0,24},{1,25},{2,26},{3,27},{4,28},{5,29},{6,30},{7,31},{8,16},{9,... | collective-permute-start | bytes 786440 | tf_op jit(solution)/shard_map/ppermute | solution.py:540
  83.3 20.2 %collective-permute-start.22 = (bf16[128,1024]{1,0:T(8,128)(2,1)S(1)}, bf16[128,1024]{1,0:T(8,128)(2,1)S(1)}, u32[]{:S(2)}, u32[]{:S(2)}) collective-permute-start(bf16[128,1024]{1,0:T(8,128)(2,1)S(1)} %get-tuple-element.255), channel_id=1, source_target_pairs={{0,25},{1,24},{2,27},{3,26},{4,29},{5,28},{6,31},{7,30},{8,17},{9,... | collective-permute-start | bytes 786440 | tf_op jit(solution)/shard_map/ppermute | solution.py:540
  93.9 3.7 %collective-permute-start.16 = (f32[1024]{0:T(1024)S(1)}, f32[1024]{0:T(1024)S(1)}, u32[]{:S(2)}, u32[]{:S(2)}) collective-permute-start(f32[1024]{0:T(1024)S(1)} %bitcast.21), channel_id=1, source_target_pairs={{0,2},{1,3},{2,0},{3,1},{4,6},{5,7},{6,4},{7,5},{8,10},{9,11},{10,... | collective-permute-start | bytes 12296 | tf_op jit(solution)/shard_map/ppermute | solution.py:448
  97.6 4.5 %collective-permute-start.17 = (f32[1024]{0:T(1024)S(1)}, f32[1024]{0:T(1024)S(1)}, u32[]{:S(2)}, u32[]{:S(2)}) collective-permute-start(f32[1024]{0:T(1024)S(1)} %max.9), channel_id=1, source_target_pairs={{0,4},{1,5},{2,6},{3,7},{4,0},{5,1},{6,2},{7,3},{8,12},{9,13},{10,... | collective-permute-start | bytes 12296 | tf_op jit(solution)/shard_map/ppermute | solution.py:448
  102.1 4.0 %collective-permute-start.18 = (f32[1024]{0:T(1024)S(1)}, f32[1024]{0:T(1024)S(1)}, u32[]{:S(2)}, u32[]{:S(2)}) collective-permute-start(f32[1024]{0:T(1024)S(1)} %max.10), channel_id=1, source_target_pairs={{0,1},{1,0},{2,3},{3,2},{4,5},{5,4},{6,7},{7,6},{8,9},{9,8},{10,11... | collective-permute-start | bytes 12296 | tf_op jit(solution)/shard_map/ppermute | solution.py:448
  (3 other events, 7.7 us)

commit v3 on v2

--- a/solution.py
+++ b/solution.py
@@ -34,9 +34,70 @@
     return jnp.dot(hot, rows, preferred_element_type=jnp.float32)
 
 
+def deal(ids, clusters, embeddings, own, cap, n_line):
+    rows, width = embeddings.shape
+    half, chunk = rows // 2, 256
+    assert own & (own - 1) == 0 and half % chunk == 0
+    spread = float(-(-rows // own))
+
+    def kernel(ids_ref, cluster_ref, rows_ref, kept_ref, given_ref, order_ref, starts_ref):
+        side, place = ids_ref[1] & 1, ids_ref[1] >> 1
+        cluster = cluster_ref[...]
+        number = lax.broadcasted_iota(jnp.int32, (1, rows), 1).astype(jnp.float32)
+        key = (cluster & -own).astype(jnp.float32) * spread + number
+        column = jnp.broadcast_to(key, (8, rows)).T[:, :1]
+        order = jnp.zeros((1, rows), jnp.float32)
+        for low in range(0, rows, chunk):
+            earlier = (column[low : low + chunk] < key).astype(jnp.float32)
+            order = order + jnp.sum(earlier, axis=0, keepdims=True)
+        order = order.astype(jnp.int32)
+        order_ref[...] = order
+        lane = lax.broadcasted_iota(jnp.int32, (1, 128), 1)
+        starts = jnp.zeros((1, 128), jnp.int32)
+        for at, step in ((ABOVE, 1), (HERE, 0), (BELOW, n_line - 1)):
+            border = (2 * lax.rem(place + step, n_line) + 1) * own
+            before = jnp.sum((cluster < border).astype(jnp.float32), axis=1, keepdims=True)
+            start = ((before.astype(jnp.int32) + 1 - side) >> 1) - cap + half
+            starts = jnp.where(lane == at, start, starts)
+            if at == ABOVE:
+                above = start
+        starts_ref[...] = starts
+        turned = (order >> 1) - above + 2 * half
+        turned = jnp.where(turned >= 2 * half, turned - 2 * half, turned)
+        turned = jnp.where(turned >= half, turned - half, turned)
+        slot = jnp.where((order & 1) == side, turned, half + (order >> 1))
+        for low in range(0, rows, chunk):
+            hit = lax.broadcasted_iota(jnp.int32, (chunk, rows), 0) + low == slot
+            found = product(hit.astype(jnp.float32).astype(jnp.bfloat16), rows_ref[...])
+            out_ref, at = (kept_ref, low) if low < half else (given_ref, low - half)
+            out_ref[at : at + chunk] = found.astype(jnp.bfloat16)
+
+    return pl.pallas_call(
+        kernel,
+        grid_spec=pltpu.PrefetchScalarGridSpec(
+            num_scalar_prefetch=1,
+            grid=(1,),
+            in_specs=[
+                pl.BlockSpec((1, rows), lambda g, ids: (0, 0)),
+                pl.BlockSpec((rows, width), lambda g, ids: (0, 0)),
+            ],
+            out_specs=[VMEM] * 4,
+        ),
+        out_shape=[
+            jax.ShapeDtypeStruct((half, width), jnp.bfloat16),
+            jax.ShapeDtypeStruct((half, width), jnp.bfloat16),
+            jax.ShapeDtypeStruct((1, rows), jnp.int32),
+            jax.ShapeDtypeStruct((1, 128), jnp.int32),
+        ],
+        compiler_params=PARAMS,
+        cost_estimate=NO_COST,
+        name="deal",
+    )(ids, clusters, embeddings)
+
+
 def between(starts_ref, has, wants, half):
-    start = 0 if has is None else starts_ref[has]
-    return lax.rem(starts_ref[wants] - start + 2 * half, half)
+    start = 0 if has is None else starts_ref[0, has]
+    return lax.rem(starts_ref[0, wants] - start + 2 * half, half)
 
 
 def turn(parts, starts, has, wants, first, count, split):
@@ -220,20 +281,21 @@
 def update(ids, rows, matches, base, prior, counts, token, divide):
     n_rows, cap = len(rows), rows[0][2].shape[0]
     feats, own = base.shape
-    width = feats // 2
+    width, n_blocks = feats // 2, 4
+    block_rows = feats // n_blocks
 
     def kernel(ids_ref, *refs):
         row_refs, match_refs = refs[:n_rows], refs[n_rows : n_rows + 2]
         base_ref, prior_ref, counts_ref, token_ref, out_ref = refs[n_rows + 2 :]
         step = pl.program_id(0)
-        for n in (0, 1):
+        for n in range(n_blocks):
 
             @pl.when(step == n)
             def _(n=n):
                 held, match = [], []
                 for (at, b, _), ref in zip(rows, row_refs):
-                    part = n ^ b
-                    held.append(ref[:, part * width : (part + 1) * width])
+                    low = ((2 * n // n_blocks) ^ b) * width + n * block_rows % width
+                    held.append(ref[:, low : low + block_rows])
                     match.append(match_refs[b][at * cap : (at + 1) * cap])
                 total = base_ref[...] + lax.dot_general(
                     jnp.concatenate(held, axis=0),
@@ -246,12 +308,15 @@
                     total = total * (1.0 / (prior_ref[...] + counts_ref[...] + nothing))
                 out_ref[...] = total
 
-    block = pl.BlockSpec((width, own), lambda g, ids: (g ^ (ids[1] & 1), 0))
+    each = n_blocks // 2
+    block = pl.BlockSpec(
+        (block_rows, own), lambda g, ids: ((g // each ^ (ids[1] & 1)) * each + g % each, 0)
+    )
     return pl.pallas_call(
         kernel,
         grid_spec=pltpu.PrefetchScalarGridSpec(
             num_scalar_prefetch=1,
-            grid=(2,),
+            grid=(n_blocks,),
             in_specs=[VMEM] * (n_rows + 2) + [block, VMEM, VMEM, VMEM],
             out_specs=block,
         ),
@@ -397,7 +462,7 @@
             column = jnp.broadcast_to(row, (8, half)).T[:, :1]
             side = ids_ref[1] & 1
             order = order_ref[...]
-            turned = (order >> 1) - starts_ref[HERE] + 2 * half
+            turned = (order >> 1) - starts_ref[0, HERE] + 2 * half
             turned = jnp.where(turned >= 2 * half, turned - 2 * half, turned)
             turned = jnp.where(turned >= half, turned - half, turned)
             ours = (order & 1) == side
@@ -448,31 +513,15 @@
         return lax.ppermute(value, "cent", pairs)
 
     ids = jnp.stack([me_dp, me])
-    owner_of = assignment // own
-    key = owner_of * rows + jnp.arange(rows, dtype=jnp.int32)
-    order = jnp.sum(key[None, :] < key[:, None], axis=1, dtype=jnp.int32)
-    parity, turn_no = order % 2, order // 2
-    layers = (place + jnp.array([1, 0, n_line - 1], jnp.int32)) % n_line
-    before = jnp.sum(owner_of[None, :] <= 2 * layers[:, None], axis=1, dtype=jnp.int32)
-    starts = (before + 1 - side) // 2 - cap + half
-    with jax.named_scope("deal_rows"):
-        slot = jnp.where(parity == side, (turn_no - starts[ABOVE] + 2 * half) % half, half + turn_no)
-        deal = jnp.arange(rows, dtype=jnp.int32)[:, None] == slot[None, :]
-        dealt = lax.dot_general(
-            deal.astype(jnp.bfloat16),
-            embeddings,
-            (((1,), (0,)), ((), ())),
-            preferred_element_type=jnp.float32,
-        ).astype(jnp.bfloat16)
+    kept, given, order, starts = deal(ids, assignment[None, :], embeddings, own, cap, n_line)
 
     steps = Steps()
     kept, given, assignment, order, centroids, ids, starts = steps.tie(
-        dealt[:half], dealt[half:], assignment, order, centroids, ids, starts
+        kept, given, assignment, order, centroids, ids, starts
     )
     up_a, swapped = send(kept, ring(1)), send(given, swap)
-    blocks = jnp.stack([assignment, order])[None]
+    blocks = jnp.stack([assignment[None, :], order], axis=1)
     prior = prior_counts.astype(jnp.float32)[None, :]
-    order = order[None, :]
     share = take_share(ids, centroids, n_dp, False)
 
     swapped, share, blocks, prior, order = steps.tie(swapped, share, blocks, prior, order)

time: 107 us -> 108 us (level)
  local copies, waits for them, and re-layouts: 0.23 us -> 4.21 us
  Pallas kernels: 26.4 us -> 30 us
  waiting for transfers between devices: 40.3 us -> 36.9 us
  other arithmetic: 3.16 us -> 1.61 us
  matrix products: 1.26 us -> 0 us
    unnamed x9 -> x10, local copies, waits for them, and re-layouts: 0.09 us -> 4.17 us
    ppermute x12, waiting for transfers between devices: 37.7 us -> 34.3 us  [send(): return lax.ppermute(value, 'cent', pairs)]
    pallas_call x0 -> x1, Pallas kernels: none -> 2.5 us  [deal(): pl.pallas_call(kernel, grid_spec=pltpu.PrefetchScalarGridSpec(num_scalar_...]
    dot_general x1 -> x0, matrix products: 1.26 us -> none  [on_device(): lax.dot_general(deal.astype(jnp.bfloat16), embeddings, (((1,), (0,)), (()...]
    pallas_call x2, Pallas kernels: 4.11 us -> 5.28 us  [update(): pl.pallas_call(kernel, grid_spec=pltpu.PrefetchScalarGridSpec(num_scalar_...]
  transfers between devices with their start and end apart: 23 -> 23, of which waited for: 11 -> 11; matrix products, arithmetic and copies ran while one was open for 0% -> 1% of each run, Pallas kernels for 24% -> 25%
where the time goes in v3:
time: 108 us
  waiting for transfers between devices  36.9 us (34%)
  starting transfers between devices  34.7 us (32%)
  Pallas kernels  30 us (28%)
  local copies, waits for them, and re-layouts  4.21 us (4%)
  other arithmetic  1.61 us (1%)
    ppermute x12, waiting for transfers between devices, send(): return lax.ppermute(value, 'cent', pairs)  34.3 us
    ppermute x12, starting transfers between devices, send(): return lax.ppermute(value, 'cent', pairs)  25.4 us
    pallas_call x2, Pallas kernels, score_part(): pl.pallas_call(kernel, grid_spec=grid_spec, out_shape=[jax.ShapeDtypeStru...  11.5 us
    ppermute x7, starting transfers between devices, deliver(): return lax.ppermute(value, ('dp', 'cent'), pairs)  6.14 us
    pallas_call x2, Pallas kernels, update(): pl.pallas_call(kernel, grid_spec=pltpu.PrefetchScalarGridSpec(num_scalar_...  5.28 us
    unnamed x10, local copies, waits for them, and re-layouts  4.17 us
    pallas_call x3, Pallas kernels, turn(): pl.pallas_call(kernel, in_specs=[SMEM] + [VMEM] * len(parts), out_specs=V...  2.94 us
    pallas_call x1, Pallas kernels, deal(): pl.pallas_call(kernel, grid_spec=pltpu.PrefetchScalarGridSpec(num_scalar_...  2.5 us
  transfers between devices with their start and end apart: 23, of which 11 were waited for; matrix products, arithmetic and copies ran while one was open for 1% of the time, Pallas kernels for 25%

profile of v3, /device:TPU:0, one launch (start us, length us, event | category | flops | bytes accessed | tf_op | source)
XLA Modules:
  0.0 108.2 jit_solution(15189871403220434115)
XLA Ops:
  2.6 2.5 %deal.1 = (bf16[512,512]{1,0:T(8,128)(2,1)S(1)}, bf16[512,512]{1,0:T(8,128)(2,1)S(1)}, s32[1,1024]{1,0:T(1,128)S(1)}, s32[1,128]{1,0:T(1,128)S(1)}) custom-call(s32[2]{0:T(128)S(1)} %pad_add_fusion.3.ids_ref, s32[1,1024]{1,0:T(1,128)S(1)} %bitcast.16, bf16[1024,512]{1,0:T(8,128)(2,1)S(1)} %copy-done.2), custom_call_target="tpu_custom_call" | custom-call | tf_op jit(solution)/shard_map/deal/pallas_call | solution.py:75
  5.1 3.0 %collective-permute-start = (bf16[512,512]{1,0:T(8,128)(2,1)S(1)}, bf16[512,512]{1,0:T(8,128)(2,1)S(1)}, u32[]{:S(2)}, u32[]{:S(2)}) collective-permute-start(bf16[512,512]{1,0:T(8,128)(2,1)S(1)} %get-tuple-element.141), channel_id=1, source_target_pairs={{0,1},{1,0},{2,3},{3,2},{4,5},{5,4},{6,7},{7,6},{8,9},{9,8},{10,11... | collective-permute-start | bytes 1572872 | tf_op jit(solution)/shard_map/ppermute | solution.py:513
  8.2 1.6 %collective-permute-start.1 = (bf16[512,512]{1,0:T(8,128)(2,1)S(1)}, bf16[512,512]{1,0:T(8,128)(2,1)S(1)}, u32[]{:S(2)}, u32[]{:S(2)}) collective-permute-start(bf16[512,512]{1,0:T(8,128)(2,1)S(1)} %get-tuple-element.149.kept_ref), channel_id=1, source_target_pairs={{0,2},{1,3},{2,4},{3,5},{4,6},{5,7},{6,0},{7,1},{8,10},{9,11},{10,... | collective-permute-start | bytes 1572872 | tf_op jit(solution)/shard_map/ppermute | solution.py:513
  10.4 2.2 %copy-done = bf16[512,4096]{1,0:T(8,128)(2,1)S(1)} copy-done((bf16[512,4096]{1,0:T(8,128)(2,1)S(1)}, bf16[512,4096]{1,0:T(8,128)(2,1)}, u32[]{:S(2)}) %copy-start) | copy-done | bytes 4194328
  13.3 6.8 %collective-permute-done.refs_0_.swapped_ref = bf16[512,512]{1,0:T(8,128)(2,1)S(1)} collective-permute-done((bf16[512,512]{1,0:T(8,128)(2,1)S(1)}, bf16[512,512]{1,0:T(8,128)(2,1)S(1)}, u32[]{:S(2)}, u32[]{:S(2)}) %collective-permute-start) | collective-permute-done | bytes 524320 | tf_op jit(solution)/shard_map/ppermute | solution.py:513
  24.2 1.6 %collective-permute-start.4 = (bf16[512,512]{1,0:T(8,128)(2,1)S(1)}, bf16[512,512]{1,0:T(8,128)(2,1)S(1)}, u32[]{:S(2)}, u32[]{:S(2)}) collective-permute-start(bf16[512,512]{1,0:T(8,128)(2,1)S(1)} %turn.3), channel_id=1, source_target_pairs={{0,2},{1,3},{2,4},{3,5},{4,6},{5,7},{6,0},{7,1},{8,10},{9,11},{10,... | collective-permute-start | bytes 1572872 | tf_op jit(solution)/shard_map/ppermute | solution.py:513
  27.2 2.2 %collective-permute-done.2 = s32[1,2,1024]{2,0,1:T(1,128)S(1)} collective-permute-done((s32[1,2,1024]{2,0,1:T(1,128)S(1)}, s32[1,2,1024]{2,0,1:T(1,128)S(1)}, u32[]{:S(2)}, u32[]{:S(2)}) %collective-permute-start.2) | collective-permute-done | bytes 8224 | tf_op jit(solution)/shard_map/ppermute | solution.py:537
  29.5 2.3 %collective-permute-start.7 = (bf16[256,1024]{1,0:T(8,128)(2,1)S(1)}, bf16[256,1024]{1,0:T(8,128)(2,1)S(1)}, u32[]{:S(2)}, u32[]{:S(2)}) collective-permute-start(bf16[256,1024]{1,0:T(8,128)(2,1)S(1)} %get-tuple-element.176), channel_id=1, source_target_pairs={{0,6},{1,7},{2,0},{3,1},{4,2},{5,3},{6,4},{7,5},{8,14},{9,15},{10,... | collective-permute-start | bytes 1572872 | tf_op jit(solution)/shard_map/ppermute | solution.py:513
  32.4 8.4 %collective-permute-done.4.refs_1_.refs_3_.refs_6_ = bf16[512,512]{1,0:T(8,128)(2,1)S(1)} collective-permute-done((bf16[512,512]{1,0:T(8,128)(2,1)S(1)}, bf16[512,512]{1,0:T(8,128)(2,1)S(1)}, u32[]{:S(2)}, u32[]{:S(2)}) %collective-permute-start.4) | collective-permute-done | bytes 524320 | tf_op jit(solution)/shard_map/ppermute | solution.py:513
  41.8 5.8 %collective-permute-start.6 = (bf16[256,1024]{1,0:T(8,128)(2,1)S(1)}, bf16[256,1024]{1,0:T(8,128)(2,1)S(1)}, u32[]{:S(2)}, u32[]{:S(2)}) collective-permute-start(bf16[256,1024]{1,0:T(8,128)(2,1)S(1)} %turn.4), channel_id=1, source_target_pairs={{0,2},{1,3},{2,4},{3,5},{4,6},{5,7},{6,0},{7,1},{8,10},{9,11},{10,... | collective-permute-start | bytes 1572872 | tf_op jit(solution)/shard_map/ppermute | solution.py:513
  49.8 2.1 %prepare.1 = (bf16[512,512]{1,0:T(8,128)(2,1)S(1)}, bf16[512,512]{1,0:T(8,128)(2,1)S(1)}, bf16[512,512]{1,0:T(8,128)(2,1)S(1)}, bf16[512,512]{1,0:T(8,128)(2,1)S...) custom-call(s32[2]{0:T(128)S(1)} %pad_add_fusion.3.ids_ref, s32[1,128]{1,0:T(1,128)S(1)} %get-tuple-element.147.starts_ref, ...), custom_call_target="tpu_custom_call" | custom-call | tf_op jit(solution)/shard_map/prepare/pallas_call | solution.py:225
  52.0 9.0 %collective-permute-done.6.refs_4_.refs_7_ = bf16[256,1024]{1,0:T(8,128)(2,1)S(1)} collective-permute-done((bf16[256,1024]{1,0:T(8,128)(2,1)S(1)}, bf16[256,1024]{1,0:T(8,128)(2,1)S(1)}, u32[]{:S(2)}, u32[]{:S(2)}) %collective-permute-start.6) | collective-permute-done | bytes 524320 | tf_op jit(solution)/shard_map/ppermute | solution.py:513
  62.1 1.8 %collective-permute-start.14 = (bf16[256,1024]{1,0:T(8,128)(2,1)S(1)}, bf16[256,1024]{1,0:T(8,128)(2,1)S(1)}, u32[]{:S(2)}, u32[]{:S(2)}) collective-permute-start(bf16[256,1024]{1,0:T(8,128)(2,1)S(1)} %get-tuple-element.223), channel_id=1, source_target_pairs={{0,6},{1,7},{2,0},{3,1},{4,2},{5,3},{6,4},{7,5},{8,14},{9,15},{10,... | collective-permute-start | bytes 1572872 | tf_op jit(solution)/shard_map/ppermute | solution.py:513
  66.3 8.3 %score_part.2 = (f32[1024,512]{1,0:T(8,128)S(1)}, f32[1,512]{1,0:T(1,128)}) custom-call(s32[2]{0:T(128)S(1)} %pad_add_fusion.3.ids_ref, bf16[512,4096]{1,0:T(8,128)(2,1)S(1)} %copy-done.1, bf16[256,4096]{1,0:T(8,128)(2,1)S(1)} %pad_maximum_fusion.refs_1_, bf16[256,4096]{1,0:T(8,128)(2,1)S(1)} %collective-permute-done.10.refs_2_, ...), custom_call_target="tpu_custom_call" | custom-call | tf_op jit(solution)/shard_map/score_part/pallas_call | solution.py:407
  74.6 1.8 %collective-permute-done.14.refs_1_.refs_4_ = bf16[256,1024]{1,0:T(8,128)(2,1)S(1)} collective-permute-done((bf16[256,1024]{1,0:T(8,128)(2,1)S(1)}, bf16[256,1024]{1,0:T(8,128)(2,1)S(1)}, u32[]{:S(2)}, u32[]{:S(2)}) %collective-permute-start.14) | collective-permute-done | bytes 524320 | tf_op jit(solution)/shard_map/ppermute | solution.py:513
  77.5 3.7 %collective-permute-start.15 = (bf16[256,1024]{1,0:T(8,128)(2,1)S(1)}, bf16[256,1024]{1,0:T(8,128)(2,1)S(1)}, u32[]{:S(2)}, u32[]{:S(2)}) collective-permute-start(bf16[256,1024]{1,0:T(8,128)(2,1)S(1)} %turn.5), channel_id=1, source_target_pairs={{0,6},{1,7},{2,0},{3,1},{4,2},{5,3},{6,4},{7,5},{8,14},{9,15},{10,... | collective-permute-start | bytes 1572872 | tf_op jit(solution)/shard_map/ppermute | solution.py:513
  85.3 3.2 %score_part.3 = (f32[1024,512]{1,0:T(8,128)S(1)}, f32[1,512]{1,0:T(1,128)S(1)}) custom-call(s32[2]{0:T(128)S(1)} %pad_add_fusion.3.ids_ref, bf16[512,4096]{1,0:T(8,128)(2,1)S(1)} %copy-done.1, bf16[256,4096]{1,0:T(8,128)(2,1)S(1)} %pad_maximum_fusion.refs_1_, bf16[256,4096]{1,0:T(8,128)(2,1)S(1)} %collective-permute-done.10.refs_2_, ...), custom_call_target="tpu_custom_call" | custom-call | tf_op jit(solution)/shard_map/score_part/pallas_call | solution.py:407
  88.5 2.0 %update.2.refs_6_ = f32[1024,512]{1,0:T(8,128)S(1)} custom-call(s32[2]{0:T(128)S(1)} %pad_add_fusion.3.ids_ref, bf16[128,1024]{1,0:T(8,128)(2,1)S(1)} %get-tuple-element.239.refs_0_, bf16[128,1024]{1,0:T(8,128)(2,1)S(1)} %collective-permute-done.11.refs_1_, bf16[128,1024]{1,0:T(8,128)(2,1)S(1)} %collective-permute-done.12.refs_2_, ...), custom_call_target="tpu_custom_call" | custom-call | tf_op jit(solution)/shard_map/update/pallas_call | solution.py:315
  90.5 1.7 %collective-permute-done.15.refs_3_ = bf16[256,1024]{1,0:T(8,128)(2,1)S(1)} collective-permute-done((bf16[256,1024]{1,0:T(8,128)(2,1)S(1)}, bf16[256,1024]{1,0:T(8,128)(2,1)S(1)}, u32[]{:S(2)}, u32[]{:S(2)}) %collective-permute-start.15) | collective-permute-done | bytes 524320 | tf_op jit(solution)/shard_map/ppermute | solution.py:513
  92.2 2.5 %score_last.1 = f32[1,1024]{1,0:T(1,128)S(1)} custom-call(s32[2]{0:T(128)S(1)} %pad_add_fusion.3.ids_ref, s32[1,128]{1,0:T(1,128)S(1)} %get-tuple-element.147.starts_ref, bf16[512,4096]{1,0:T(8,128)(2,1)S(1)} %copy-done.1, bf16[256,4096]{1,0:T(8,128)(2,1)S(1)} %pad_maximum_fusion.refs_1_, bf16[256,4096]{1,0:T(8,128)(2,1)S(1)} %collective-permute-done.10.refs_2_, ...), custom_call_target="tpu_custom_call" | custom-call | tf_op jit(solution)/shard_map/score_last/pallas_call | solution.py:486
  94.8 3.6 %collective-permute-done.16 = f32[1024]{0:T(1024)S(1)} collective-permute-done((f32[1024]{0:T(1024)S(1)}, f32[1024]{0:T(1024)S(1)}, u32[]{:S(2)}, u32[]{:S(2)}) %collective-permute-start.16) | collective-permute-done | bytes 4128 | tf_op jit(solution)/shard_map/ppermute | solution.py:513
  98.4 2.8 %collective-permute-start.17 = (f32[1024]{0:T(1024)S(1)}, f32[1024]{0:T(1024)S(1)}, u32[]{:S(2)}, u32[]{:S(2)}) collective-permute-start(f32[1024]{0:T(1024)S(1)} %max.9), channel_id=1, source_target_pairs={{0,4},{1,5},{2,6},{3,7},{4,0},{5,1},{6,2},{7,3},{8,12},{9,13},{10,... | collective-permute-start | bytes 12296 | tf_op jit(solution)/shard_map/ppermute | solution.py:513
  101.2 1.7 %collective-permute-done.17 = f32[1024]{0:T(1024)S(1)} collective-permute-done((f32[1024]{0:T(1024)S(1)}, f32[1024]{0:T(1024)S(1)}, u32[]{:S(2)}, u32[]{:S(2)}) %collective-permute-start.17) | collective-permute-done | bytes 4128 | tf_op jit(solution)/shard_map/ppermute | solution.py:513
  104.3 3.3 %update.3 = f32[1024,512]{1,0:T(8,128)} custom-call(s32[2]{0:T(128)S(1)} %pad_add_fusion.3.ids_ref, bf16[128,1024]{1,0:T(8,128)(2,1)S(1)} %collective-permute-done.21.refs_0_, bf16[128,1024]{1,0:T(8,128)(2,1)S(1)} %collective-permute-done.19.refs_1_, bf16[128,1024]{1,0:T(8,128)(2,1)S(1)} %collective-permute-done.20.refs_2_, ...), custom_call_target="tpu_custom_call" | custom-call | tf_op jit(solution)/shard_map/update/pallas_call | solution.py:315
  (58 shorter events, 23.5 us)
Async XLA Ops:
  5.1 15.0 %collective-permute-start = (bf16[512,512]{1,0:T(8,128)(2,1)S(1)}, bf16[512,512]{1,0:T(8,128)(2,1)S(1)}, u32[]{:S(2)}, u32[]{:S(2)}) collective-permute-start(bf16[512,512]{1,0:T(8,128)(2,1)S(1)} %get-tuple-element.141), channel_id=1, source_target_pairs={{0,1},{1,0},{2,3},{3,2},{4,5},{5,4},{6,7},{7,6},{8,9},{9,8},{10,11... | collective-permute-start | bytes 1572872 | tf_op jit(solution)/shard_map/ppermute | solution.py:513
  8.2 15.2 %collective-permute-start.1 = (bf16[512,512]{1,0:T(8,128)(2,1)S(1)}, bf16[512,512]{1,0:T(8,128)(2,1)S(1)}, u32[]{:S(2)}, u32[]{:S(2)}) collective-permute-start(bf16[512,512]{1,0:T(8,128)(2,1)S(1)} %get-tuple-element.149.kept_ref), channel_id=1, source_target_pairs={{0,2},{1,3},{2,4},{3,5},{4,6},{5,7},{6,0},{7,1},{8,10},{9,11},{10,... | collective-permute-start | bytes 1572872 | tf_op jit(solution)/shard_map/ppermute | solution.py:513
  12.6 19.2 %copy-start.1 = (bf16[512,4096]{1,0:T(8,128)(2,1)S(1)}, bf16[512,4096]{1,0:T(8,128)(2,1)}, u32[]{:S(2)}) copy-start(bf16[512,4096]{1,0:T(8,128)(2,1)} %refs_0_.2) | copy-start | bytes 12582916
  23.4 24.2 %collective-permute-start.5 = (bf16[128,4096]{1,0:T(8,128)(2,1)S(1)}, bf16[128,4096]{1,0:T(8,128)(2,1)S(1)}, u32[]{:S(2)}, u32[]{:S(2)}) collective-permute-start(bf16[128,4096]{1,0:T(8,128)(2,1)S(1)} %take_share.2), channel_id=1, source_target_pairs={{0,1},{1,0},{2,3},{3,2},{4,5},{5,4},{6,7},{7,6},{8,9},{9,8},{10,11... | collective-permute-start | bytes 3145736 | tf_op jit(solution)/shard_map/ppermute | solution.py:513
  24.2 16.7 %collective-permute-start.4 = (bf16[512,512]{1,0:T(8,128)(2,1)S(1)}, bf16[512,512]{1,0:T(8,128)(2,1)S(1)}, u32[]{:S(2)}, u32[]{:S(2)}) collective-permute-start(bf16[512,512]{1,0:T(8,128)(2,1)S(1)} %turn.3), channel_id=1, source_target_pairs={{0,2},{1,3},{2,4},{3,5},{4,6},{5,7},{6,0},{7,1},{8,10},{9,11},{10,... | collective-permute-start | bytes 1572872 | tf_op jit(solution)/shard_map/ppermute | solution.py:513
  25.7 3.7 %collective-permute-start.2 = (s32[1,2,1024]{2,0,1:T(1,128)S(1)}, s32[1,2,1024]{2,0,1:T(1,128)S(1)}, u32[]{:S(2)}, u32[]{:S(2)}) collective-permute-start(s32[1,2,1024]{2,0,1:T(1,128)S(1)} %pad_add_fusion.2), channel_id=1, source_target_pairs={{0,16},{8,24},{16,0},{24,8},{1,17},{9,25},{17,1},{25,9},{2,18},{10... | collective-permute-start | bytes 24584 | tf_op jit(solution)/shard_map/ppermute | solution.py:537
  29.4 2.4 %collective-permute-start.3 = (s32[2,2,1024]{2,0,1:T(2,128)S(1)}, s32[2,2,1024]{2,0,1:T(2,128)S(1)}, u32[]{:S(2)}, u32[]{:S(2)}) collective-permute-start(s32[2,2,1024]{2,0,1:T(2,128)S(1)} %pad_add_fusion.1), channel_id=1, source_target_pairs={{0,8},{8,0},{16,24},{24,16},{1,9},{9,1},{17,25},{25,17},{2,10},{10... | collective-permute-start | bytes 49160 | tf_op jit(solution)/shard_map/ppermute | solution.py:537
  29.5 22.5 %collective-permute-start.7 = (bf16[256,1024]{1,0:T(8,128)(2,1)S(1)}, bf16[256,1024]{1,0:T(8,128)(2,1)S(1)}, u32[]{:S(2)}, u32[]{:S(2)}) collective-permute-start(bf16[256,1024]{1,0:T(8,128)(2,1)S(1)} %get-tuple-element.176), channel_id=1, source_target_pairs={{0,6},{1,7},{2,0},{3,1},{4,2},{5,3},{6,4},{7,5},{8,14},{9,15},{10,... | collective-permute-start | bytes 1572872 | tf_op jit(solution)/shard_map/ppermute | solution.py:513
  41.8 19.2 %collective-permute-start.6 = (bf16[256,1024]{1,0:T(8,128)(2,1)S(1)}, bf16[256,1024]{1,0:T(8,128)(2,1)S(1)}, u32[]{:S(2)}, u32[]{:S(2)}) collective-permute-start(bf16[256,1024]{1,0:T(8,128)(2,1)S(1)} %turn.4), channel_id=1, source_target_pairs={{0,2},{1,3},{2,4},{3,5},{4,6},{5,7},{6,0},{7,1},{8,10},{9,11},{10,... | collective-permute-start | bytes 1572872 | tf_op jit(solution)/shard_map/ppermute | solution.py:513
  47.7 14.1 %collective-permute-start.8 = (bf16[64,4096]{1,0:T(8,128)(2,1)S(1)}, bf16[64,4096]{1,0:T(8,128)(2,1)S(1)}, u32[]{:S(2)}, u32[]{:S(2)}) collective-permute-start(bf16[64,4096]{1,0:T(8,128)(2,1)S(1)} %slice.11), channel_id=1, source_target_pairs={{0,16},{8,24},{16,0},{24,8},{1,17},{9,25},{17,1},{25,9},{2,18},{10... | collective-permute-start | bytes 1572872 | tf_op jit(solution)/shard_map/ppermute | solution.py:561
  49.3 12.6 %collective-permute-start.9 = (bf16[64,4096]{1,0:T(8,128)(2,1)S(1)}, bf16[64,4096]{1,0:T(8,128)(2,1)S(1)}, u32[]{:S(2)}, u32[]{:S(2)}) collective-permute-start(bf16[64,4096]{1,0:T(8,128)(2,1)S(1)} %take_share.3), channel_id=1, source_target_pairs={{0,1},{1,0},{2,3},{3,2},{4,5},{5,4},{6,7},{7,6},{8,9},{9,8},{10,11... | collective-permute-start | bytes 1572872 | tf_op jit(solution)/shard_map/ppermute | solution.py:513
  62.1 4.2 %collective-permute-start.10 = (bf16[256,4096]{1,0:T(8,128)(2,1)S(1)}, bf16[256,4096]{1,0:T(8,128)(2,1)S(1)}, u32[]{:S(2)}, u32[]{:S(2)}) collective-permute-start(bf16[256,4096]{1,0:T(8,128)(2,1)S(1)} %pad_maximum_fusion.refs_1_), channel_id=1, source_target_pairs={{0,8},{8,0},{16,24},{24,16},{1,9},{9,1},{17,25},{25,17},{2,10},{10... | collective-permute-start | bytes 6291464 | tf_op jit(solution)/shard_map/ppermute | solution.py:603
  62.1 14.3 %collective-permute-start.14 = (bf16[256,1024]{1,0:T(8,128)(2,1)S(1)}, bf16[256,1024]{1,0:T(8,128)(2,1)S(1)}, u32[]{:S(2)}, u32[]{:S(2)}) collective-permute-start(bf16[256,1024]{1,0:T(8,128)(2,1)S(1)} %get-tuple-element.223), channel_id=1, source_target_pairs={{0,6},{1,7},{2,0},{3,1},{4,2},{5,3},{6,4},{7,5},{8,14},{9,15},{10,... | collective-permute-start | bytes 1572872 | tf_op jit(solution)/shard_map/ppermute | solution.py:513
  63.9 10.7 %collective-permute-start.11 = (bf16[128,1024]{1,0:T(8,128)(2,1)S(1)}, bf16[128,1024]{1,0:T(8,128)(2,1)S(1)}, u32[]{:S(2)}, u32[]{:S(2)}) collective-permute-start(bf16[128,1024]{1,0:T(8,128)(2,1)S(1)} %get-tuple-element.219), channel_id=1, source_target_pairs={{0,16},{1,17},{2,18},{3,19},{4,20},{5,21},{6,22},{7,23},{8,24},{9,... | collective-permute-start | bytes 786440 | tf_op jit(solution)/shard_map/ppermute | solution.py:589
  65.4 9.2 %collective-permute-start.12 = (bf16[128,1024]{1,0:T(8,128)(2,1)S(1)}, bf16[128,1024]{1,0:T(8,128)(2,1)S(1)}, u32[]{:S(2)}, u32[]{:S(2)}) collective-permute-start(bf16[128,1024]{1,0:T(8,128)(2,1)S(1)} %get-tuple-element.220), channel_id=1, source_target_pairs={{0,1},{1,0},{2,3},{3,2},{4,5},{5,4},{6,7},{7,6},{8,9},{9,8},{10,11... | collective-permute-start | bytes 786440 | tf_op jit(solution)/shard_map/ppermute | solution.py:589
  65.9 8.7 %collective-permute-start.13 = (bf16[128,1024]{1,0:T(8,128)(2,1)S(1)}, bf16[128,1024]{1,0:T(8,128)(2,1)S(1)}, u32[]{:S(2)}, u32[]{:S(2)}) collective-permute-start(bf16[128,1024]{1,0:T(8,128)(2,1)S(1)} %get-tuple-element.221), channel_id=1, source_target_pairs={{0,8},{1,9},{2,10},{3,11},{4,12},{5,13},{6,14},{7,15},{8,0},{9,1},... | collective-permute-start | bytes 786440 | tf_op jit(solution)/shard_map/ppermute | solution.py:589
  77.5 14.7 %collective-permute-start.15 = (bf16[256,1024]{1,0:T(8,128)(2,1)S(1)}, bf16[256,1024]{1,0:T(8,128)(2,1)S(1)}, u32[]{:S(2)}, u32[]{:S(2)}) collective-permute-start(bf16[256,1024]{1,0:T(8,128)(2,1)S(1)} %turn.5), channel_id=1, source_target_pairs={{0,6},{1,7},{2,0},{3,1},{4,2},{5,3},{6,4},{7,5},{8,14},{9,15},{10,... | collective-permute-start | bytes 1572872 | tf_op jit(solution)/shard_map/ppermute | solution.py:513
  81.2 23.1 %collective-permute-start.19 = (bf16[128,1024]{1,0:T(8,128)(2,1)S(1)}, bf16[128,1024]{1,0:T(8,128)(2,1)S(1)}, u32[]{:S(2)}, u32[]{:S(2)}) collective-permute-start(bf16[128,1024]{1,0:T(8,128)(2,1)S(1)} %get-tuple-element.260), channel_id=1, source_target_pairs={{0,9},{1,8},{2,11},{3,10},{4,13},{5,12},{6,15},{7,14},{8,1},{9,0},... | collective-permute-start | bytes 786440 | tf_op jit(solution)/shard_map/ppermute | solution.py:589
  81.6 22.7 %collective-permute-start.20 = (bf16[128,1024]{1,0:T(8,128)(2,1)S(1)}, bf16[128,1024]{1,0:T(8,128)(2,1)S(1)}, u32[]{:S(2)}, u32[]{:S(2)}) collective-permute-start(bf16[128,1024]{1,0:T(8,128)(2,1)S(1)} %get-tuple-element.261), channel_id=1, source_target_pairs={{0,17},{1,16},{2,19},{3,18},{4,21},{5,20},{6,23},{7,22},{8,25},{9,... | collective-permute-start | bytes 786440 | tf_op jit(solution)/shard_map/ppermute | solution.py:589
  83.1 21.2 %collective-permute-start.21 = (bf16[128,1024]{1,0:T(8,128)(2,1)S(1)}, bf16[128,1024]{1,0:T(8,128)(2,1)S(1)}, u32[]{:S(2)}, u32[]{:S(2)}) collective-permute-start(bf16[128,1024]{1,0:T(8,128)(2,1)S(1)} %get-tuple-element.262), channel_id=1, source_target_pairs={{0,24},{1,25},{2,26},{3,27},{4,28},{5,29},{6,30},{7,31},{8,16},{9,... | collective-permute-start | bytes 786440 | tf_op jit(solution)/shard_map/ppermute | solution.py:589
  84.1 20.2 %collective-permute-start.22 = (bf16[128,1024]{1,0:T(8,128)(2,1)S(1)}, bf16[128,1024]{1,0:T(8,128)(2,1)S(1)}, u32[]{:S(2)}, u32[]{:S(2)}) collective-permute-start(bf16[128,1024]{1,0:T(8,128)(2,1)S(1)} %get-tuple-element.263), channel_id=1, source_target_pairs={{0,25},{1,24},{2,27},{3,26},{4,29},{5,28},{6,31},{7,30},{8,17},{9,... | collective-permute-start | bytes 786440 | tf_op jit(solution)/shard_map/ppermute | solution.py:589
  94.7 3.7 %collective-permute-start.16 = (f32[1024]{0:T(1024)S(1)}, f32[1024]{0:T(1024)S(1)}, u32[]{:S(2)}, u32[]{:S(2)}) collective-permute-start(f32[1024]{0:T(1024)S(1)} %bitcast.14), channel_id=1, source_target_pairs={{0,2},{1,3},{2,0},{3,1},{4,6},{5,7},{6,4},{7,5},{8,10},{9,11},{10,... | collective-permute-start | bytes 12296 | tf_op jit(solution)/shard_map/ppermute | solution.py:513
  98.4 4.5 %collective-permute-start.17 = (f32[1024]{0:T(1024)S(1)}, f32[1024]{0:T(1024)S(1)}, u32[]{:S(2)}, u32[]{:S(2)}) collective-permute-start(f32[1024]{0:T(1024)S(1)} %max.9), channel_id=1, source_target_pairs={{0,4},{1,5},{2,6},{3,7},{4,0},{5,1},{6,2},{7,3},{8,12},{9,13},{10,... | collective-permute-start | bytes 12296 | tf_op jit(solution)/shard_map/ppermute | solution.py:513
  102.9 4.7 %collective-permute-start.18 = (f32[1024]{0:T(1024)S(1)}, f32[1024]{0:T(1024)S(1)}, u32[]{:S(2)}, u32[]{:S(2)}) collective-permute-start(f32[1024]{0:T(1024)S(1)} %max.10), channel_id=1, source_target_pairs={{0,1},{1,0},{2,3},{3,2},{4,5},{5,4},{6,7},{7,6},{8,9},{9,8},{10,11... | collective-permute-start | bytes 12296 | tf_op jit(solution)/shard_map/ppermute | solution.py:513
  (4 other events, 4.8 us)

commit v4 on v2

--- a/solution.py
+++ b/solution.py
@@ -225,17 +225,18 @@
     def kernel(ids_ref, *refs):
         row_refs, match_refs = refs[:n_rows], refs[n_rows : n_rows + 2]
         base_ref, prior_ref, counts_ref, token_ref, out_ref = refs[n_rows + 2 :]
-        step = pl.program_id(0)
-        for n in (0, 1):
-
-            @pl.when(step == n)
-            def _(n=n):
+        for side in (0, 1):
+
+            @pl.when(ids_ref[1] & 1 == side)
+            def _(side=side):
+              for n in (0, 1):
+                low = (n ^ side) * width
                 held, match = [], []
                 for (at, b, _), ref in zip(rows, row_refs):
                     part = n ^ b
                     held.append(ref[:, part * width : (part + 1) * width])
                     match.append(match_refs[b][at * cap : (at + 1) * cap])
-                total = base_ref[...] + lax.dot_general(
+                total = base_ref[low : low + width] + lax.dot_general(
                     jnp.concatenate(held, axis=0),
                     jnp.concatenate(match, axis=0),
                     (((0,), (0,)), ((), ())),
@@ -244,15 +245,15 @@
                 if divide:
                     nothing = token_ref[:1, :1].astype(jnp.float32)
                     total = total * (1.0 / (prior_ref[...] + counts_ref[...] + nothing))
-                out_ref[...] = total
-
-    block = pl.BlockSpec((width, own), lambda g, ids: (g ^ (ids[1] & 1), 0))
+                out_ref[low : low + width] = total
+
+    block = pl.BlockSpec((feats, own), lambda g, ids: (0, 0))
     return pl.pallas_call(
         kernel,
         grid_spec=pltpu.PrefetchScalarGridSpec(
             num_scalar_prefetch=1,
-            grid=(2,),
-            in_specs=[VMEM] * (n_rows + 2) + [block, VMEM, VMEM, VMEM],
+            grid=(1,),
+            in_specs=[VMEM] * (n_rows + 6),
             out_specs=block,
         ),
         out_shape=jax.ShapeDtypeStruct((feats, own), jnp.float32),
@@ -365,56 +366,56 @@
         score_refs = refs[n_tables + 1 : n_tables + 1 + n_scores]
         best_refs = refs[n_tables + 1 + n_scores : n_tables + 1 + 2 * n_scores]
         order_ref, out_ref, piece, sums = refs[n_tables + 1 + 2 * n_scores :]
-        step = pl.program_id(0)
         if low_row < near:
-            piece[: near - low_row] = jnp.zeros((near - low_row, width), piece.dtype)
-        for n in (0, 1):
-
-            @pl.when(step == n)
-            def _(n=n):
-                piece[near - low_row :] = last_ref[:, n * width : (n + 1) * width]
+            piece[: near - low_row] = jnp.zeros((near - low_row, 2 * width), piece.dtype)
+        for side in (0, 1):
+
+            @pl.when(ids_ref[1] & 1 == side)
+            def _(side=side):
+                for n in (0, 1):
+                    low = (side ^ n) * width
+                    part = last_ref[:, n * width : (n + 1) * width]
+                    piece[near - low_row :, low : low + width] = part
 
         low = 0
         for ref, size in zip(table_refs, sizes):
-            part = lax.dot_general(
+            sums[low : low + size] = lax.dot_general(
                 ref[...], piece[...], (((1,), (1,)), ((), ())), preferred_element_type=jnp.float32
             )
-            sums[low : low + size] = part + jnp.where(step == 0, 0.0, sums[low : low + size])
             low += size
 
-        @pl.when(step == 1)
-        def _():
-            late, low = [], 0
-            for ref in score_refs:
-                high = low + ref.shape[0]
-                score = sums[low:high] + ref[:, low_row:]
-                late.append(jnp.max(score, axis=0, keepdims=True))
-                low = high
-            row = largest_of(late)
-            if low_row:
-                first = largest_of([ref[:, :low_row] for ref in best_refs])
-                row = jnp.concatenate([first, row], axis=1)
-            column = jnp.broadcast_to(row, (8, half)).T[:, :1]
-            side = ids_ref[1] & 1
-            order = order_ref[...]
-            turned = (order >> 1) - starts_ref[HERE] + 2 * half
-            turned = jnp.where(turned >= 2 * half, turned - 2 * half, turned)
-            turned = jnp.where(turned >= half, turned - half, turned)
-            ours = (order & 1) == side
-            found = lax.broadcasted_iota(jnp.int32, (half, rows), 0) == turned
-            best = jnp.sum(jnp.where(found, column, 0.0), axis=0, keepdims=True)
-            out_ref[...] = jnp.where(ours, best, -jnp.inf)
+        late, low = [], 0
+        for ref in score_refs:
+            high = low + ref.shape[0]
+            score = sums[low:high] + ref[:, low_row:]
+            late.append(jnp.max(score, axis=0, keepdims=True))
+            low = high
+        row = largest_of(late)
+        if low_row:
+            first = largest_of([ref[:, :low_row] for ref in best_refs])
+            row = jnp.concatenate([first, row], axis=1)
+        column = jnp.broadcast_to(row, (8, half)).T[:, :1]
+        side = ids_ref[1] & 1
+        order = order_ref[...]
+        turned = (order >> 1) - starts_ref[HERE] + 2 * half
+        turned = jnp.where(turned >= 2 * half, turned - 2 * half, turned)
+        turned = jnp.where(turned >= half, turned - half, turned)
+        ours = (order & 1) == side
+        found = lax.broadcasted_iota(jnp.int32, (half, rows), 0) == turned
+        best = jnp.sum(jnp.where(found, column, 0.0), axis=0, keepdims=True)
+        out_ref[...] = jnp.where(ours, best, -jnp.inf)
 
     grid_spec = pltpu.PrefetchScalarGridSpec(
         num_scalar_prefetch=2,
-        grid=(2,),
+        grid=(1,),
         in_specs=[
-            pl.BlockSpec((size, width), lambda g, ids, at: (0, block(g, ids))) for size in sizes
+            pl.BlockSpec((size, 2 * width), lambda g, ids, at: (0, block(g, ids) // 2))
+            for size in sizes
         ]
         + [VMEM] * (2 + 2 * n_scores),
         out_specs=VMEM,
         scratch_shapes=[
-            pltpu.VMEM((half - low_row, width), jnp.bfloat16),
+            pltpu.VMEM((half - low_row, 2 * width), jnp.bfloat16),
             pltpu.VMEM((total, half - low_row), jnp.float32),
         ],
     )
@@ -548,10 +549,12 @@
         windows[n_line - step] = (down[0],)
     first = [(2, 0), (0, 1), (1, 0)]
     second = [(m, 0) for m in range(3, n_dp)] + [(m, 1) for m in range(1, n_dp)]
-    got = steps.tie(collect(ids, [windows[n] for n in range(n_line)], cap, n_dp))
     others = steps.tie(others)
     core_sent = steps.tie(jnp.concatenate(others, axis=0))
     core = lax.ppermute(core_sent, "dp", [(d, d ^ 1) for d in range(n_dp)])
+    middle_near, close = steps.tie(middle_near, close)
+    windows[middle], windows[n_line - 1] = (middle_near,), (close,)
+    got = steps.tie(collect(ids, [windows[n] for n in range(n_line)], cap, n_dp))
     for key in first:
         got[key] = deliver(got[key], *key)
 

time: 107 us -> 106 us (level)
  waiting for transfers between devices: 40.3 us -> 38.9 us
  starting transfers between devices: 34.5 us -> 35.7 us
    ppermute x12, starting transfers between devices: 25.2 us -> 26.6 us  [send(): return lax.ppermute(value, 'cent', pairs)]
  transfers between devices with their start and end apart: 23 -> 23, of which waited for: 11 -> 10; matrix products, arithmetic and copies ran while one was open for 0% -> 0% of each run, Pallas kernels for 24% -> 23%
where the time goes in v4:
time: 106 us
  waiting for transfers between devices  38.9 us (37%)
  starting transfers between devices  35.7 us (34%)
  Pallas kernels  25.8 us (24%)
  other arithmetic  3.19 us (3%)
  matrix products  1.26 us (1%)
    ppermute x12, waiting for transfers between devices, send(): return lax.ppermute(value, 'cent', pairs)  36.8 us
    ppermute x12, starting transfers between devices, send(): return lax.ppermute(value, 'cent', pairs)  26.6 us
    pallas_call x2, Pallas kernels, score_part(): pl.pallas_call(kernel, grid_spec=grid_spec, out_shape=[jax.ShapeDtypeStru...  11.5 us
    ppermute x7, starting transfers between devices, deliver(): return lax.ppermute(value, ('dp', 'cent'), pairs)  6.01 us
    pallas_call x2, Pallas kernels, update(): pl.pallas_call(kernel, grid_spec=pltpu.PrefetchScalarGridSpec(num_scalar_...  4.2 us
    pallas_call x3, Pallas kernels, turn(): pl.pallas_call(kernel, in_specs=[SMEM] + [VMEM] * len(parts), out_specs=V...  2.94 us
    ppermute x2, waiting for transfers between devices, on_device(): lax.ppermute(blocks, 'dp', pairs)  2.15 us
  transfers between devices with their start and end apart: 23, of which 10 were waited for; matrix products, arithmetic and copies ran while one was open for 0% of the time, Pallas kernels for 23%

profile of v4, /device:TPU:0, one launch (start us, length us, event | category | flops | bytes accessed | tf_op | source)
XLA Modules:
  0.0 106.0 jit_solution(1945635725600161484)
XLA Ops:
  4.4 3.0 %collective-permute-start = (bf16[512,512]{1,0:T(8,128)(2,1)S(1)}, bf16[512,512]{1,0:T(8,128)(2,1)S(1)}, u32[]{:S(2)}, u32[]{:S(2)}) collective-permute-start(bf16[512,512]{1,0:T(8,128)(2,1)S(1)} %get-tuple-element.136), channel_id=1, source_target_pairs={{0,1},{1,0},{2,3},{3,2},{4,5},{5,4},{6,7},{7,6},{8,9},{9,8},{10,11... | collective-permute-start | bytes 1572872 | tf_op jit(solution)/shard_map/ppermute | solution.py:449
  7.4 1.6 %collective-permute-start.1 = (bf16[512,512]{1,0:T(8,128)(2,1)S(1)}, bf16[512,512]{1,0:T(8,128)(2,1)S(1)}, u32[]{:S(2)}, u32[]{:S(2)}) collective-permute-start(bf16[512,512]{1,0:T(8,128)(2,1)S(1)} %get-tuple-element.144.kept_ref), channel_id=1, source_target_pairs={{0,2},{1,3},{2,4},{3,5},{4,6},{5,7},{6,0},{7,1},{8,10},{9,11},{10,... | collective-permute-start | bytes 1572872 | tf_op jit(solution)/shard_map/ppermute | solution.py:449
  9.7 9.6 %collective-permute-done.refs_0_.swapped_ref = bf16[512,512]{1,0:T(8,128)(2,1)S(1)} collective-permute-done((bf16[512,512]{1,0:T(8,128)(2,1)S(1)}, bf16[512,512]{1,0:T(8,128)(2,1)S(1)}, u32[]{:S(2)}, u32[]{:S(2)}) %collective-permute-start) | collective-permute-done | bytes 524320 | tf_op jit(solution)/shard_map/ppermute | solution.py:449
  23.4 1.6 %collective-permute-start.4 = (bf16[512,512]{1,0:T(8,128)(2,1)S(1)}, bf16[512,512]{1,0:T(8,128)(2,1)S(1)}, u32[]{:S(2)}, u32[]{:S(2)}) collective-permute-start(bf16[512,512]{1,0:T(8,128)(2,1)S(1)} %turn.3), channel_id=1, source_target_pairs={{0,2},{1,3},{2,4},{3,5},{4,6},{5,7},{6,0},{7,1},{8,10},{9,11},{10,... | collective-permute-start | bytes 1572872 | tf_op jit(solution)/shard_map/ppermute | solution.py:449
  24.9 1.5 %collective-permute-start.2 = (s32[1,2,1024]{2,1,0:T(2,128)S(1)}, s32[1,2,1024]{2,1,0:T(2,128)S(1)}, u32[]{:S(2)}, u32[]{:S(2)}) collective-permute-start(s32[1,2,1024]{2,1,0:T(2,128)S(1)} %add_bitcast_fusion), channel_id=1, source_target_pairs={{0,16},{8,24},{16,0},{24,8},{1,17},{9,25},{17,1},{25,9},{2,18},{10... | collective-permute-start | bytes 24584 | tf_op jit(solution)/shard_map/ppermute | solution.py:489
  26.4 2.1 %collective-permute-done.2 = s32[1,2,1024]{2,1,0:T(2,128)S(1)} collective-permute-done((s32[1,2,1024]{2,1,0:T(2,128)S(1)}, s32[1,2,1024]{2,1,0:T(2,128)S(1)}, u32[]{:S(2)}, u32[]{:S(2)}) %collective-permute-start.2) | collective-permute-done | bytes 8224 | tf_op jit(solution)/shard_map/ppermute | solution.py:489
  28.6 2.3 %collective-permute-start.7 = (bf16[256,1024]{1,0:T(8,128)(2,1)S(1)}, bf16[256,1024]{1,0:T(8,128)(2,1)S(1)}, u32[]{:S(2)}, u32[]{:S(2)}) collective-permute-start(bf16[256,1024]{1,0:T(8,128)(2,1)S(1)} %get-tuple-element.171), channel_id=1, source_target_pairs={{0,6},{1,7},{2,0},{3,1},{4,2},{5,3},{6,4},{7,5},{8,14},{9,15},{10,... | collective-permute-start | bytes 1572872 | tf_op jit(solution)/shard_map/ppermute | solution.py:449
  31.5 8.6 %collective-permute-done.4.refs_1_.refs_3_.refs_6_ = bf16[512,512]{1,0:T(8,128)(2,1)S(1)} collective-permute-done((bf16[512,512]{1,0:T(8,128)(2,1)S(1)}, bf16[512,512]{1,0:T(8,128)(2,1)S(1)}, u32[]{:S(2)}, u32[]{:S(2)}) %collective-permute-start.4) | collective-permute-done | bytes 524320 | tf_op jit(solution)/shard_map/ppermute | solution.py:449
  41.1 5.8 %collective-permute-start.6 = (bf16[256,1024]{1,0:T(8,128)(2,1)S(1)}, bf16[256,1024]{1,0:T(8,128)(2,1)S(1)}, u32[]{:S(2)}, u32[]{:S(2)}) collective-permute-start(bf16[256,1024]{1,0:T(8,128)(2,1)S(1)} %turn.4), channel_id=1, source_target_pairs={{0,2},{1,3},{2,4},{3,5},{4,6},{5,7},{6,0},{7,1},{8,10},{9,11},{10,... | collective-permute-start | bytes 1572872 | tf_op jit(solution)/shard_map/ppermute | solution.py:449
  46.9 1.5 %collective-permute-start.8 = (bf16[64,4096]{1,0:T(8,128)(2,1)S(1)}, bf16[64,4096]{1,0:T(8,128)(2,1)S(1)}, u32[]{:S(2)}, u32[]{:S(2)}) collective-permute-start(bf16[64,4096]{1,0:T(8,128)(2,1)S(1)} %slice.23), channel_id=1, source_target_pairs={{0,16},{8,24},{16,0},{24,8},{1,17},{9,25},{17,1},{25,9},{2,18},{10... | collective-permute-start | bytes 1572872 | tf_op jit(solution)/shard_map/ppermute | solution.py:513
  49.0 2.1 %prepare.1 = (bf16[512,512]{1,0:T(8,128)(2,1)S(1)}, bf16[512,512]{1,0:T(8,128)(2,1)S(1)}, bf16[512,512]{1,0:T(8,128)(2,1)S(1)}, bf16[512,512]{1,0:T(8,128)(2,1)S...) custom-call(s32[2]{0:T(128)S(1)} %pad_add_fusion.2.ids_ref, s32[3]{0:T(128)S(1)} %fusion.12.starts_ref, ...), custom_call_target="tpu_custom_call" | custom-call | tf_op jit(solution)/shard_map/prepare/pallas_call | solution.py:164
  51.2 9.0 %collective-permute-done.6.refs_4_.refs_7_ = bf16[256,1024]{1,0:T(8,128)(2,1)S(1)} collective-permute-done((bf16[256,1024]{1,0:T(8,128)(2,1)S(1)}, bf16[256,1024]{1,0:T(8,128)(2,1)S(1)}, u32[]{:S(2)}, u32[]{:S(2)}) %collective-permute-start.6) | collective-permute-done | bytes 524320 | tf_op jit(solution)/shard_map/ppermute | solution.py:449
  60.6 2.4 %collective-permute-start.14 = (bf16[256,1024]{1,0:T(8,128)(2,1)S(1)}, bf16[256,1024]{1,0:T(8,128)(2,1)S(1)}, u32[]{:S(2)}, u32[]{:S(2)}) collective-permute-start(bf16[256,1024]{1,0:T(8,128)(2,1)S(1)} %get-tuple-element.221), channel_id=1, source_target_pairs={{0,6},{1,7},{2,0},{3,1},{4,2},{5,3},{6,4},{7,5},{8,14},{9,15},{10,... | collective-permute-start | bytes 1572872 | tf_op jit(solution)/shard_map/ppermute | solution.py:449
  65.9 8.3 %score_part.2 = (f32[1024,512]{1,0:T(8,128)S(1)}, f32[1,512]{1,0:T(1,128)}) custom-call(s32[2]{0:T(128)S(1)} %pad_add_fusion.2.ids_ref, bf16[512,4096]{1,0:T(8,128)(2,1)S(1)} %copy-done.1, bf16[256,4096]{1,0:T(8,128)(2,1)S(1)} %pad_maximum_fusion.refs_1_, bf16[256,4096]{1,0:T(8,128)(2,1)S(1)} %collective-permute-done.10.refs_2_, ...), custom_call_target="tpu_custom_call" | custom-call | tf_op jit(solution)/shard_map/score_part/pallas_call | solution.py:343
  75.9 4.2 %collective-permute-start.15 = (bf16[256,1024]{1,0:T(8,128)(2,1)S(1)}, bf16[256,1024]{1,0:T(8,128)(2,1)S(1)}, u32[]{:S(2)}, u32[]{:S(2)}) collective-permute-start(bf16[256,1024]{1,0:T(8,128)(2,1)S(1)} %turn.5), channel_id=1, source_target_pairs={{0,6},{1,7},{2,0},{3,1},{4,2},{5,3},{6,4},{7,5},{8,14},{9,15},{10,... | collective-permute-start | bytes 1572872 | tf_op jit(solution)/shard_map/ppermute | solution.py:449
  84.0 3.2 %score_part.3 = (f32[1024,512]{1,0:T(8,128)S(1)}, f32[1,512]{1,0:T(1,128)S(1)}) custom-call(s32[2]{0:T(128)S(1)} %pad_add_fusion.2.ids_ref, bf16[512,4096]{1,0:T(8,128)(2,1)S(1)} %copy-done.1, bf16[256,4096]{1,0:T(8,128)(2,1)S(1)} %pad_maximum_fusion.refs_1_, bf16[256,4096]{1,0:T(8,128)(2,1)S(1)} %collective-permute-done.10.refs_2_, ...), custom_call_target="tpu_custom_call" | custom-call | tf_op jit(solution)/shard_map/score_part/pallas_call | solution.py:343
  87.2 1.5 %update.2.refs_6_ = f32[1024,512]{1,0:T(8,128)S(1)} custom-call(s32[2]{0:T(128)S(1)} %pad_add_fusion.2.ids_ref, bf16[128,1024]{1,0:T(8,128)(2,1)S(1)} %get-tuple-element.237.refs_0_, bf16[128,1024]{1,0:T(8,128)(2,1)S(1)} %collective-permute-done.11.refs_1_, bf16[128,1024]{1,0:T(8,128)(2,1)S(1)} %collective-permute-done.12.refs_2_, ...), custom_call_target="tpu_custom_call" | custom-call | tf_op jit(solution)/shard_map/update/pallas_call | solution.py:251
  88.7 2.4 %collective-permute-done.15.refs_3_ = bf16[256,1024]{1,0:T(8,128)(2,1)S(1)} collective-permute-done((bf16[256,1024]{1,0:T(8,128)(2,1)S(1)}, bf16[256,1024]{1,0:T(8,128)(2,1)S(1)}, u32[]{:S(2)}, u32[]{:S(2)}) %collective-permute-start.15) | collective-permute-done | bytes 524320 | tf_op jit(solution)/shard_map/ppermute | solution.py:449
  91.1 1.8 %score_last.1 = f32[1,1024]{1,0:T(1,128)S(1)} custom-call(s32[2]{0:T(128)S(1)} %pad_add_fusion.2.ids_ref, s32[3]{0:T(128)S(1)} %fusion.12.starts_ref, bf16[512,4096]{1,0:T(8,128)(2,1)S(1)} %copy-done.1, bf16[256,4096]{1,0:T(8,128)(2,1)S(1)} %pad_maximum_fusion.refs_1_, bf16[256,4096]{1,0:T(8,128)(2,1)S(1)} %collective-permute-done.10.refs_2_, ...), custom_call_target="tpu_custom_call" | custom-call | tf_op jit(solution)/shard_map/score_last/pallas_call | solution.py:422
  93.0 3.6 %collective-permute-done.16 = f32[1024]{0:T(1024)S(1)} collective-permute-done((f32[1024]{0:T(1024)S(1)}, f32[1024]{0:T(1024)S(1)}, u32[]{:S(2)}, u32[]{:S(2)}) %collective-permute-start.16) | collective-permute-done | bytes 4128 | tf_op jit(solution)/shard_map/ppermute | solution.py:449
  96.6 2.8 %collective-permute-start.17 = (f32[1024]{0:T(1024)S(1)}, f32[1024]{0:T(1024)S(1)}, u32[]{:S(2)}, u32[]{:S(2)}) collective-permute-start(f32[1024]{0:T(1024)S(1)} %max.9), channel_id=1, source_target_pairs={{0,4},{1,5},{2,6},{3,7},{4,0},{5,1},{6,2},{7,3},{8,12},{9,13},{10,... | collective-permute-start | bytes 12296 | tf_op jit(solution)/shard_map/ppermute | solution.py:449
  99.5 1.7 %collective-permute-done.17 = f32[1024]{0:T(1024)S(1)} collective-permute-done((f32[1024]{0:T(1024)S(1)}, f32[1024]{0:T(1024)S(1)}, u32[]{:S(2)}, u32[]{:S(2)}) %collective-permute-start.17) | collective-permute-done | bytes 4128 | tf_op jit(solution)/shard_map/ppermute | solution.py:449
  101.1 1.5 %collective-permute-start.18 = (f32[1024]{0:T(1024)S(1)}, f32[1024]{0:T(1024)S(1)}, u32[]{:S(2)}, u32[]{:S(2)}) collective-permute-start(f32[1024]{0:T(1024)S(1)} %max.10), channel_id=1, source_target_pairs={{0,1},{1,0},{2,3},{3,2},{4,5},{5,4},{6,7},{7,6},{8,9},{9,8},{10,11... | collective-permute-start | bytes 12296 | tf_op jit(solution)/shard_map/ppermute | solution.py:449
  102.7 2.7 %update.3 = f32[1024,512]{1,0:T(8,128)} custom-call(s32[2]{0:T(128)S(1)} %pad_add_fusion.2.ids_ref, bf16[128,1024]{1,0:T(8,128)(2,1)S(1)} %collective-permute-done.21.refs_0_, bf16[128,1024]{1,0:T(8,128)(2,1)S(1)} %collective-permute-done.19.refs_1_, bf16[128,1024]{1,0:T(8,128)(2,1)S(1)} %collective-permute-done.20.refs_2_, ...), custom_call_target="tpu_custom_call" | custom-call | tf_op jit(solution)/shard_map/update/pallas_call | solution.py:251
  (64 shorter events, 20.1 us)
Async XLA Ops:
  3.0 6.0 %copy-start.1 = (bf16[512,4096]{1,0:T(8,128)(2,1)S(1)}, bf16[512,4096]{1,0:T(8,128)(2,1)}, u32[]{:S(2)}) copy-start(bf16[512,4096]{1,0:T(8,128)(2,1)} %refs_0_.2) | copy-start | bytes 12582916
  4.4 14.9 %collective-permute-start = (bf16[512,512]{1,0:T(8,128)(2,1)S(1)}, bf16[512,512]{1,0:T(8,128)(2,1)S(1)}, u32[]{:S(2)}, u32[]{:S(2)}) collective-permute-start(bf16[512,512]{1,0:T(8,128)(2,1)S(1)} %get-tuple-element.136), channel_id=1, source_target_pairs={{0,1},{1,0},{2,3},{3,2},{4,5},{5,4},{6,7},{7,6},{8,9},{9,8},{10,11... | collective-permute-start | bytes 1572872 | tf_op jit(solution)/shard_map/ppermute | solution.py:449
  7.4 15.2 %collective-permute-start.1 = (bf16[512,512]{1,0:T(8,128)(2,1)S(1)}, bf16[512,512]{1,0:T(8,128)(2,1)S(1)}, u32[]{:S(2)}, u32[]{:S(2)}) collective-permute-start(bf16[512,512]{1,0:T(8,128)(2,1)S(1)} %get-tuple-element.144.kept_ref), channel_id=1, source_target_pairs={{0,2},{1,3},{2,4},{3,5},{4,6},{5,7},{6,0},{7,1},{8,10},{9,11},{10,... | collective-permute-start | bytes 1572872 | tf_op jit(solution)/shard_map/ppermute | solution.py:449
  22.6 24.3 %collective-permute-start.5 = (bf16[128,4096]{1,0:T(8,128)(2,1)S(1)}, bf16[128,4096]{1,0:T(8,128)(2,1)S(1)}, u32[]{:S(2)}, u32[]{:S(2)}) collective-permute-start(bf16[128,4096]{1,0:T(8,128)(2,1)S(1)} %take_share.2), channel_id=1, source_target_pairs={{0,1},{1,0},{2,3},{3,2},{4,5},{5,4},{6,7},{7,6},{8,9},{9,8},{10,11... | collective-permute-start | bytes 3145736 | tf_op jit(solution)/shard_map/ppermute | solution.py:449
  23.4 16.7 %collective-permute-start.4 = (bf16[512,512]{1,0:T(8,128)(2,1)S(1)}, bf16[512,512]{1,0:T(8,128)(2,1)S(1)}, u32[]{:S(2)}, u32[]{:S(2)}) collective-permute-start(bf16[512,512]{1,0:T(8,128)(2,1)S(1)} %turn.3), channel_id=1, source_target_pairs={{0,2},{1,3},{2,4},{3,5},{4,6},{5,7},{6,0},{7,1},{8,10},{9,11},{10,... | collective-permute-start | bytes 1572872 | tf_op jit(solution)/shard_map/ppermute | solution.py:449
  24.9 3.7 %collective-permute-start.2 = (s32[1,2,1024]{2,1,0:T(2,128)S(1)}, s32[1,2,1024]{2,1,0:T(2,128)S(1)}, u32[]{:S(2)}, u32[]{:S(2)}) collective-permute-start(s32[1,2,1024]{2,1,0:T(2,128)S(1)} %add_bitcast_fusion), channel_id=1, source_target_pairs={{0,16},{8,24},{16,0},{24,8},{1,17},{9,25},{17,1},{25,9},{2,18},{10... | collective-permute-start | bytes 24584 | tf_op jit(solution)/shard_map/ppermute | solution.py:489
  28.6 2.3 %collective-permute-start.3 = (s32[2,2,1024]{2,1,0:T(2,128)S(1)}, s32[2,2,1024]{2,1,0:T(2,128)S(1)}, u32[]{:S(2)}, u32[]{:S(2)}) collective-permute-start(s32[2,2,1024]{2,1,0:T(2,128)S(1)} %pad_add_fusion.1), channel_id=1, source_target_pairs={{0,8},{8,0},{16,24},{24,16},{1,9},{9,1},{17,25},{25,17},{2,10},{10... | collective-permute-start | bytes 49160 | tf_op jit(solution)/shard_map/ppermute | solution.py:489
  28.6 22.6 %collective-permute-start.7 = (bf16[256,1024]{1,0:T(8,128)(2,1)S(1)}, bf16[256,1024]{1,0:T(8,128)(2,1)S(1)}, u32[]{:S(2)}, u32[]{:S(2)}) collective-permute-start(bf16[256,1024]{1,0:T(8,128)(2,1)S(1)} %get-tuple-element.171), channel_id=1, source_target_pairs={{0,6},{1,7},{2,0},{3,1},{4,2},{5,3},{6,4},{7,5},{8,14},{9,15},{10,... | collective-permute-start | bytes 1572872 | tf_op jit(solution)/shard_map/ppermute | solution.py:449
  41.1 19.2 %collective-permute-start.6 = (bf16[256,1024]{1,0:T(8,128)(2,1)S(1)}, bf16[256,1024]{1,0:T(8,128)(2,1)S(1)}, u32[]{:S(2)}, u32[]{:S(2)}) collective-permute-start(bf16[256,1024]{1,0:T(8,128)(2,1)S(1)} %turn.4), channel_id=1, source_target_pairs={{0,2},{1,3},{2,4},{3,5},{4,6},{5,7},{6,0},{7,1},{8,10},{9,11},{10,... | collective-permute-start | bytes 1572872 | tf_op jit(solution)/shard_map/ppermute | solution.py:449
  46.9 13.3 %collective-permute-start.8 = (bf16[64,4096]{1,0:T(8,128)(2,1)S(1)}, bf16[64,4096]{1,0:T(8,128)(2,1)S(1)}, u32[]{:S(2)}, u32[]{:S(2)}) collective-permute-start(bf16[64,4096]{1,0:T(8,128)(2,1)S(1)} %slice.23), channel_id=1, source_target_pairs={{0,16},{8,24},{16,0},{24,8},{1,17},{9,25},{17,1},{25,9},{2,18},{10... | collective-permute-start | bytes 1572872 | tf_op jit(solution)/shard_map/ppermute | solution.py:513
  48.5 11.8 %collective-permute-start.9 = (bf16[64,4096]{1,0:T(8,128)(2,1)S(1)}, bf16[64,4096]{1,0:T(8,128)(2,1)S(1)}, u32[]{:S(2)}, u32[]{:S(2)}) collective-permute-start(bf16[64,4096]{1,0:T(8,128)(2,1)S(1)} %take_share.3), channel_id=1, source_target_pairs={{0,1},{1,0},{2,3},{3,2},{4,5},{5,4},{6,7},{7,6},{8,9},{9,8},{10,11... | collective-permute-start | bytes 1572872 | tf_op jit(solution)/shard_map/ppermute | solution.py:449
  60.5 5.5 %collective-permute-start.10 = (bf16[256,4096]{1,0:T(8,128)(2,1)S(1)}, bf16[256,4096]{1,0:T(8,128)(2,1)S(1)}, u32[]{:S(2)}, u32[]{:S(2)}) collective-permute-start(bf16[256,4096]{1,0:T(8,128)(2,1)S(1)} %pad_maximum_fusion.refs_1_), channel_id=1, source_target_pairs={{0,8},{8,0},{16,24},{24,16},{1,9},{9,1},{17,25},{25,17},{2,10},{10... | collective-permute-start | bytes 6291464 | tf_op jit(solution)/shard_map/ppermute | solution.py:554
  60.6 14.3 %collective-permute-start.14 = (bf16[256,1024]{1,0:T(8,128)(2,1)S(1)}, bf16[256,1024]{1,0:T(8,128)(2,1)S(1)}, u32[]{:S(2)}, u32[]{:S(2)}) collective-permute-start(bf16[256,1024]{1,0:T(8,128)(2,1)S(1)} %get-tuple-element.221), channel_id=1, source_target_pairs={{0,6},{1,7},{2,0},{3,1},{4,2},{5,3},{6,4},{7,5},{8,14},{9,15},{10,... | collective-permute-start | bytes 1572872 | tf_op jit(solution)/shard_map/ppermute | solution.py:449
  63.8 10.5 %collective-permute-start.11 = (bf16[128,1024]{1,0:T(8,128)(2,1)S(1)}, bf16[128,1024]{1,0:T(8,128)(2,1)S(1)}, u32[]{:S(2)}, u32[]{:S(2)}) collective-permute-start(bf16[128,1024]{1,0:T(8,128)(2,1)S(1)} %get-tuple-element.217), channel_id=1, source_target_pairs={{0,16},{1,17},{2,18},{3,19},{4,20},{5,21},{6,22},{7,23},{8,24},{9,... | collective-permute-start | bytes 786440 | tf_op jit(solution)/shard_map/ppermute | solution.py:541
  64.6 9.6 %collective-permute-start.12 = (bf16[128,1024]{1,0:T(8,128)(2,1)S(1)}, bf16[128,1024]{1,0:T(8,128)(2,1)S(1)}, u32[]{:S(2)}, u32[]{:S(2)}) collective-permute-start(bf16[128,1024]{1,0:T(8,128)(2,1)S(1)} %get-tuple-element.218), channel_id=1, source_target_pairs={{0,1},{1,0},{2,3},{3,2},{4,5},{5,4},{6,7},{7,6},{8,9},{9,8},{10,11... | collective-permute-start | bytes 786440 | tf_op jit(solution)/shard_map/ppermute | solution.py:541
  65.9 8.4 %collective-permute-start.13 = (bf16[128,1024]{1,0:T(8,128)(2,1)S(1)}, bf16[128,1024]{1,0:T(8,128)(2,1)S(1)}, u32[]{:S(2)}, u32[]{:S(2)}) collective-permute-start(bf16[128,1024]{1,0:T(8,128)(2,1)S(1)} %get-tuple-element.219), channel_id=1, source_target_pairs={{0,8},{1,9},{2,10},{3,11},{4,12},{5,13},{6,14},{7,15},{8,0},{9,1},... | collective-permute-start | bytes 786440 | tf_op jit(solution)/shard_map/ppermute | solution.py:541
  75.9 15.2 %collective-permute-start.15 = (bf16[256,1024]{1,0:T(8,128)(2,1)S(1)}, bf16[256,1024]{1,0:T(8,128)(2,1)S(1)}, u32[]{:S(2)}, u32[]{:S(2)}) collective-permute-start(bf16[256,1024]{1,0:T(8,128)(2,1)S(1)} %turn.5), channel_id=1, source_target_pairs={{0,6},{1,7},{2,0},{3,1},{4,2},{5,3},{6,4},{7,5},{8,14},{9,15},{10,... | collective-permute-start | bytes 1572872 | tf_op jit(solution)/shard_map/ppermute | solution.py:449
  80.1 22.6 %collective-permute-start.19 = (bf16[128,1024]{1,0:T(8,128)(2,1)S(1)}, bf16[128,1024]{1,0:T(8,128)(2,1)S(1)}, u32[]{:S(2)}, u32[]{:S(2)}) collective-permute-start(bf16[128,1024]{1,0:T(8,128)(2,1)S(1)} %get-tuple-element.258), channel_id=1, source_target_pairs={{0,9},{1,8},{2,11},{3,10},{4,13},{5,12},{6,15},{7,14},{8,1},{9,0},... | collective-permute-start | bytes 786440 | tf_op jit(solution)/shard_map/ppermute | solution.py:541
  80.6 22.1 %collective-permute-start.20 = (bf16[128,1024]{1,0:T(8,128)(2,1)S(1)}, bf16[128,1024]{1,0:T(8,128)(2,1)S(1)}, u32[]{:S(2)}, u32[]{:S(2)}) collective-permute-start(bf16[128,1024]{1,0:T(8,128)(2,1)S(1)} %get-tuple-element.259), channel_id=1, source_target_pairs={{0,17},{1,16},{2,19},{3,18},{4,21},{5,20},{6,23},{7,22},{8,25},{9,... | collective-permute-start | bytes 786440 | tf_op jit(solution)/shard_map/ppermute | solution.py:541
  81.6 21.1 %collective-permute-start.21 = (bf16[128,1024]{1,0:T(8,128)(2,1)S(1)}, bf16[128,1024]{1,0:T(8,128)(2,1)S(1)}, u32[]{:S(2)}, u32[]{:S(2)}) collective-permute-start(bf16[128,1024]{1,0:T(8,128)(2,1)S(1)} %get-tuple-element.260), channel_id=1, source_target_pairs={{0,24},{1,25},{2,26},{3,27},{4,28},{5,29},{6,30},{7,31},{8,16},{9,... | collective-permute-start | bytes 786440 | tf_op jit(solution)/shard_map/ppermute | solution.py:541
  83.0 19.6 %collective-permute-start.22 = (bf16[128,1024]{1,0:T(8,128)(2,1)S(1)}, bf16[128,1024]{1,0:T(8,128)(2,1)S(1)}, u32[]{:S(2)}, u32[]{:S(2)}) collective-permute-start(bf16[128,1024]{1,0:T(8,128)(2,1)S(1)} %get-tuple-element.261), channel_id=1, source_target_pairs={{0,25},{1,24},{2,27},{3,26},{4,29},{5,28},{6,31},{7,30},{8,17},{9,... | collective-permute-start | bytes 786440 | tf_op jit(solution)/shard_map/ppermute | solution.py:541
  93.0 3.7 %collective-permute-start.16 = (f32[1024]{0:T(1024)S(1)}, f32[1024]{0:T(1024)S(1)}, u32[]{:S(2)}, u32[]{:S(2)}) collective-permute-start(f32[1024]{0:T(1024)S(1)} %bitcast.21), channel_id=1, source_target_pairs={{0,2},{1,3},{2,0},{3,1},{4,6},{5,7},{6,4},{7,5},{8,10},{9,11},{10,... | collective-permute-start | bytes 12296 | tf_op jit(solution)/shard_map/ppermute | solution.py:449
  96.6 4.5 %collective-permute-start.17 = (f32[1024]{0:T(1024)S(1)}, f32[1024]{0:T(1024)S(1)}, u32[]{:S(2)}, u32[]{:S(2)}) collective-permute-start(f32[1024]{0:T(1024)S(1)} %max.9), channel_id=1, source_target_pairs={{0,4},{1,5},{2,6},{3,7},{4,0},{5,1},{6,2},{7,3},{8,12},{9,13},{10,... | collective-permute-start | bytes 12296 | tf_op jit(solution)/shard_map/ppermute | solution.py:449
  101.1 4.2 %collective-permute-start.18 = (f32[1024]{0:T(1024)S(1)}, f32[1024]{0:T(1024)S(1)}, u32[]{:S(2)}, u32[]{:S(2)}) collective-permute-start(f32[1024]{0:T(1024)S(1)} %max.10), channel_id=1, source_target_pairs={{0,1},{1,0},{2,3},{3,2},{4,5},{5,4},{6,7},{7,6},{8,9},{9,8},{10,11... | collective-permute-start | bytes 12296 | tf_op jit(solution)/shard_map/ppermute | solution.py:449
  (3 other events, 7.7 us)
